TPU v7x, 32 devices: a whole 2x2x4 slice. The times are simulated.
32 devices in a mesh: nodes: 8 (over y, x, core), states: 4 (over z).
Axes of the slice: x: 2, y: 2, z: 4, core: 2. Of those that a mesh axis runs over, the one named last changes fastest.
Arguments:
- states_block: float32 [128, 4096], P('states', 'nodes'), may hold values from -6 to 6
- hamiltonian: bfloat16 [64, 64, 1728], P('nodes'), may hold values from -0.15625 to 0.15625
- offsets: int32 [64, 27], P('nodes'), may hold values from -4 to 4, as said below
- center: float32 [1], replicated, may hold values from -0.5 to 0.5
- halfwidth: float32 [1], replicated, may hold values from 0.8 to 1.6
Outputs:
- rotated: float32 [128, 4096], P('states', 'nodes')
Inputs may be any that keep to these rules, and one draw needn't show every extreme that they name: `offsets`: the first entry of every row is 0; the values -4 and 4 occur in every draw.
All inputs are finite; a program needn't handle non-finite values.
Results may differ from a plain program's by a relative error of at most 0.0003.
Values may be sent and summed in bfloat16 or wider, within the bound.
No kernel may reach another device: no remote copies, remote signals or barrier semaphores. Data moves between devices by JAX's collectives and lax.ppermute only.
A program may use at most 64 MiB of HBM per device.

v0:
```python
import jax
import jax.numpy as jnp
from jax import lax
from jax.sharding import PartitionSpec as P

REACH = 4


def with_halo(cells, sides, width):
    for axis, dim in sides:
        count = lax.axis_size(axis)
        head = lax.slice_in_dim(cells, 0, width, axis=dim)
        tail = lax.slice_in_dim(cells, cells.shape[dim] - width, cells.shape[dim], axis=dim)
        cells = jnp.concatenate(
            [
                lax.ppermute(tail, axis, [(i, (i + 1) % count) for i in range(count)]),
                cells,
                lax.ppermute(head, axis, [((i + 1) % count, i) for i in range(count)]),
            ],
            axis=dim,
        )
    return cells


def apply_local(extended, hamiltonian, offsets, lead):
    count = hamiltonian.shape[0]
    size = hamiltonian.shape[1]
    local_states = extended.shape[0]
    blocked = extended.reshape(local_states, extended.shape[1] // size, size)
    index = jnp.arange(count, dtype=jnp.int32)[:, None] + lead + offsets
    picked = blocked[:, index].reshape(local_states, count, hamiltonian.shape[2])
    result = jnp.einsum(
        "bim,cbm->cbi", hamiltonian.astype(jnp.float32), picked, precision=lax.Precision.HIGHEST
    )
    return result.reshape(local_states, count * size)


def on_device(states_block, hamiltonian, offsets, center, halfwidth):
    shift = center[0]
    width = halfwidth[0]
    size = hamiltonian.shape[1]
    reach = REACH
    rim = reach * size

    def filter_step(field):
        extended = with_halo(field, (("nodes", 1),), rim)
        return apply_local(extended, hamiltonian, offsets, reach)

    first = (filter_step(states_block) - shift * states_block) / width
    second = 2.0 * (filter_step(first) - shift * first) / width - states_block
    total_nodes = second.shape[1] * lax.axis_size("nodes")
    local_states = second.shape[0]
    all_states = local_states * lax.axis_size("states")
    identity = jnp.eye(all_states, dtype=jnp.float32)
    gathered = lax.all_gather(second, "states", axis=0, tiled=True)
    terms = jnp.dot(gathered, gathered.T, precision=lax.Precision.HIGHEST)
    intersection = lax.psum(terms, "nodes") / total_nodes
    lower = jnp.linalg.cholesky(intersection)
    inverse = lax.linalg.triangular_solve(lower, identity, left_side=True, lower=True)
    mine = lax.dynamic_slice_in_dim(
        inverse, lax.axis_index("states") * local_states, local_states, 0
    )
    return jnp.dot(mine, gathered, precision=lax.Precision.HIGHEST)


def solution(mesh):
    placed = (P("states", "nodes"), P("nodes", None, None), P("nodes", None), P(), P())
    return jax.shard_map(
        on_device, mesh=mesh, in_specs=placed, out_specs=P("states", "nodes"), check_vma=False
    )
```

profile of v0, /device:TPU:0, one launch (start us, length us, event | category | flops | bytes accessed | tf_op | source)
XLA Modules:
  0.0 154.1 jit_solution(14481846275960685863)
XLA Ops:
  6.5 0.9 fusion.8
  7.9 2.9 %collective-permute-start.1 = (f32[32,256]{1,0:T(8,128)S(1)}, f32[32,256]{1,0:T(8,128)S(1)}, u32[]{:S(2)}, u32[]{:S(2)}) collective-permute-start(f32[32,256]{1,0:T(8,128)S(1)} %get-tuple-element.8), channel_id=1, source_target_pairs={{4,0},{8,4},{12,8},{16,12},{20,16},{24,20},{28,24},{0,28},{5,1},{9... | collective-permute-start | bytes 98312 | tf_op jit(solution)/shard_map/ppermute | solution.py:18
  10.8 0.8 compare_select_fusion
  13.0 0.9 pad_maximum_fusion
  14.1 2.8 %gather_fusion = f32[216,32,64]{2,1,0:T(8,128)} fusion(f32[32,16,64]{2,0,1:T(8,128)S(1)} %copy.18, s32[1024]{0:T(1024)S(1)} %pad_clamp_fusion), kind=kCustom, calls=%fused_computation | custom fusion | bytes 3539808 | tf_op jit(solution)/shard_map/gather | solution.py:31
  16.8 6.0 %copy.29 = f32[32,8,27,64]{3,2,0,1:T(8,128)} copy(f32[32,8,27,64]{3,0,2,1:T(8,128)} %bitcast.37) | data formatting | bytes 3538944 | tf_op jit(solution)/shard_map/reshape | solution.py:31
  22.8 4.7 %reshape.58 = f32[32,8,1728]{2,0,1:T(8,128)} reshape(f32[32,8,27,64]{3,2,0,1:T(8,128)} %copy.29) | data formatting | bytes 3538944 | tf_op jit(solution)/shard_map/reshape | solution.py:31
  27.5 3.1 %convolution_bitcast_fusion.1 = f32[32,8,64]{2,0,1:T(8,128)S(1)} fusion(f32[32,8,1728]{2,0,1:T(8,128)} %reshape.58, bf16[8,64,1728]{2,1,0:T(8,128)(2,1)S(1)} %copy-done), kind=kOutput, calls=%fused_computation.3 | convolution fusion | flops 339738624 | bytes 3604480 | tf_op jit(solution)/shard_map/bim,cbm->cbi/dot_general | solution.py:32
  30.8 0.9 collective-permute-start.2
  31.6 1.8 %collective-permute-start.3 = (f32[32,256]{1,0:T(8,128)S(1)}, f32[32,256]{1,0:T(8,128)S(1)}, u32[]{:S(2)}, u32[]{:S(2)}) collective-permute-start(f32[32,256]{1,0:T(8,128)S(1)} %get-tuple-element.6), channel_id=1, source_target_pairs={{4,0},{8,4},{12,8},{16,12},{20,16},{24,20},{28,24},{0,28},{5,1},{9... | collective-permute-start | bytes 98312 | tf_op jit(solution)/shard_map/ppermute | solution.py:18
  33.5 1.6 %collective-permute-done.2 = f32[32,256]{1,0:T(8,128)S(1)} collective-permute-done((f32[32,256]{1,0:T(8,128)S(1)}, f32[32,256]{1,0:T(8,128)S(1)}, u32[]{:S(2)}, u32[]{:S(2)}) %collective-permute-start.2) | collective-permute-done | bytes 32800 | tf_op jit(solution)/shard_map/ppermute | solution.py:16
  35.3 2.8 %gather_fusion.1 = f32[216,32,64]{2,1,0:T(8,128)} fusion(f32[32,16,64]{2,0,1:T(8,128)S(1)} %copy.22, s32[1024]{0:T(1024)S(1)} %pad_clamp_fusion), kind=kCustom, calls=%fused_computation.1 | custom fusion | bytes 3539808 | tf_op jit(solution)/shard_map/gather | solution.py:31
  38.0 6.0 %copy.30 = f32[32,8,27,64]{3,2,0,1:T(8,128)} copy(f32[32,8,27,64]{3,0,2,1:T(8,128)} %bitcast.36) | data formatting | bytes 3538944 | tf_op jit(solution)/shard_map/reshape | solution.py:31
  44.0 4.7 %reshape.59 = f32[32,8,1728]{2,0,1:T(8,128)} reshape(f32[32,8,27,64]{3,2,0,1:T(8,128)} %copy.30) | data formatting | bytes 3538944 | tf_op jit(solution)/shard_map/reshape | solution.py:31
  48.7 3.0 %convolution_bitcast_fusion = f32[32,8,64]{2,0,1:T(8,128)S(1)} fusion(f32[32,8,1728]{2,0,1:T(8,128)} %reshape.59, bf16[8,64,1728]{2,1,0:T(8,128)(2,1)S(1)} %copy-done), kind=kOutput, calls=%fused_computation.2 | convolution fusion | flops 339738624 | bytes 3604480 | tf_op jit(solution)/shard_map/bim,cbm->cbi/dot_general | solution.py:32
  51.9 14.9 %all_gather.3 = f32[128,512]{1,0:T(8,128)S(1)} all-gather(f32[32,512]{1,0:T(8,128)S(1)} %divide_subtract_fusion), channel_id=1, replica_groups=mesh['nodes'=8,'states'=4] {'states'}, dimensions={0}, use_global_device_ids=true | all-gather | bytes 327680 | tf_op jit(solution)/shard_map/all_gather | solution.py:55
  66.8 1.0 fusion.9
  67.9 53.6 %all-reduce.2.cloned.1.call-done = f32[128,128]{0,1:T(8,128)} async-done(((f32[128,128]{0,1:T(8,128)}), f32[128,128]{0,1:T(8,128)}) %all-reduce.2.cloned.1.call-update) | async-done | bytes 65552 | tf_op jit(solution)/shard_map/psum | solution.py:57
  121.5 0.8 broadcast_multiply_fusion
  122.4 0.9 fusion.3
  123.3 11.7 %cholesky.17 = f32[128,128]{1,0:T(8,128)S(1)} custom-call(f32[128,128]{1,0:T(8,128)S(1)} %fusion.3), custom_call_target="Cholesky" | custom-call | tf_op jit(solution)/shard_map/jit(cholesky)/cholesky | solution.py:58
  135.7 0.7 fusion
  136.3 9.8 %custom-call.6 = f32[1,128,128]{1,2,0:T(8,128)S(1)} custom-call(f32[1,128,128]{2,1,0:T(8,128)S(1)} %fusion), custom_call_target="InvertDiagBlocksLowerTriangular" | custom-call | tf_op jit(solution)/shard_map/triangular_solve | solution.py:59
  146.4 0.9 fusion.4
  (29 shorter events, 2.4 us)
Async XLA Ops:
  6.5 20.9 %copy-start = (bf16[8,64,1728]{2,1,0:T(8,128)(2,1)S(1)}, bf16[8,64,1728]{2,1,0:T(8,128)(2,1)}, u32[]{:S(2)}) copy-start(bf16[8,64,1728]{2,1,0:T(8,128)(2,1)} %param.6) | copy-start | bytes 5308420
  6.5 114.9 %all-reduce.2.cloned.1.call-start = ((), (), s32[]{:S(2)}) async-start(), calls=%async_computation | async-start | bytes 131072 | tf_op jit(solution)/shard_map/psum | solution.py:57
  7.5 5.5 %collective-permute-start = (f32[32,256]{1,0:T(8,128)S(1)}, f32[32,256]{1,0:T(8,128)S(1)}, u32[]{:S(2)}, u32[]{:S(2)}) collective-permute-start(f32[32,256]{1,0:T(8,128)S(1)} %get-tuple-element.7), channel_id=1, source_target_pairs={{0,4},{4,8},{8,12},{12,16},{16,20},{20,24},{24,28},{28,0},{1,5},{5... | collective-permute-start | bytes 98312 | tf_op jit(solution)/shard_map/ppermute | solution.py:16
  7.9 5.1 %collective-permute-start.1 = (f32[32,256]{1,0:T(8,128)S(1)}, f32[32,256]{1,0:T(8,128)S(1)}, u32[]{:S(2)}, u32[]{:S(2)}) collective-permute-start(f32[32,256]{1,0:T(8,128)S(1)} %get-tuple-element.8), channel_id=1, source_target_pairs={{4,0},{8,4},{12,8},{16,12},{20,16},{24,20},{28,24},{0,28},{5,1},{9... | collective-permute-start | bytes 98312 | tf_op jit(solution)/shard_map/ppermute | solution.py:18
  27.5 3.3 %copy-start.1 = (f32[32,512]{1,0:T(8,128)S(1)}, f32[32,512]{1,0:T(8,128)}, u32[]{:S(2)}) copy-start(f32[32,512]{1,0:T(8,128)} %param.5) | copy-start | bytes 196612
  30.8 4.3 %collective-permute-start.2 = (f32[32,256]{1,0:T(8,128)S(1)}, f32[32,256]{1,0:T(8,128)S(1)}, u32[]{:S(2)}, u32[]{:S(2)}) collective-permute-start(f32[32,256]{1,0:T(8,128)S(1)} %get-tuple-element.5), channel_id=1, source_target_pairs={{0,4},{4,8},{8,12},{12,16},{16,20},{20,24},{24,28},{28,0},{1,5},{5... | collective-permute-start | bytes 98312 | tf_op jit(solution)/shard_map/ppermute | solution.py:16
  31.6 3.4 %collective-permute-start.3 = (f32[32,256]{1,0:T(8,128)S(1)}, f32[32,256]{1,0:T(8,128)S(1)}, u32[]{:S(2)}, u32[]{:S(2)}) collective-permute-start(f32[32,256]{1,0:T(8,128)S(1)} %get-tuple-element.6), channel_id=1, source_target_pairs={{4,0},{8,4},{12,8},{16,12},{20,16},{24,20},{28,24},{0,28},{5,1},{9... | collective-permute-start | bytes 98312 | tf_op jit(solution)/shard_map/ppermute | solution.py:18
Sparse Core Ops, SparseCore 0:
  68.0 53.4 all-reduce.1
where the time goes:
time: 155 us; the launch traced here: 154 us
  waiting for transfers between devices  55.2 us (36%)
  local copies, waits for them, and re-layouts  28.6 us (18%)
  other arithmetic  26.2 us (17%)
  blocking collectives  14.9 us (10%)
  between operations  14.8 us (10%)
  matrix products  8.27 us (5%)
  starting transfers between devices  6.09 us (4%)
    psum x1, waiting for transfers between devices, on_device(): intersection = lax.psum(terms, 'nodes') / total_nodes  53.6 us
    reshape x4, local copies, waits for them, and re-layouts, apply_local(): blocked[:, index].reshape(local_states, count, hamiltonian.shape[2])  21.3 us
    all_gather x1, blocking collectives, on_device(): gathered = lax.all_gather(second, 'states', axis=0, tiled=True)  14.9 us
    another operation x3, other arithmetic, on_device(): lower = jnp.linalg.cholesky(intersection)  12.4 us
    another operation x2, other arithmetic, on_device(): lax.linalg.triangular_solve(lower, identity, left_side=True, lower=True)  10.5 us
    dot_general x2, matrix products, apply_local(): jnp.einsum('bim,cbm->cbi', hamiltonian.astype(jnp.float32), picked, preci...  6.11 us
    gather x2, local copies, waits for them, and re-layouts, apply_local(): blocked[:, index].reshape(local_states, count, hamiltonian.shape[2])  5.52 us
    ppermute x2, starting transfers between devices, with_halo(): lax.ppermute(head, axis, [((i + 1) % count, i) for i in range(count)])  4.76 us
  transfers between devices with their start and end apart: 5, of which 2 were waited for; matrix products, arithmetic and copies ran while one was open for 1% of the time, Pallas kernels for 0%

commit v1 on v0

v1 whole, which is shorter than its diff:
```python
import functools

import jax
import jax.numpy as jnp
from jax import lax
from jax.experimental import pallas as pl
from jax.experimental.pallas import tpu as pltpu
from jax.sharding import PartitionSpec as P

REACH = 4
LANES = 128
PANEL = 16
VMEM = pl.BlockSpec(memory_space=pltpu.VMEM)
SMEM = pl.BlockSpec(memory_space=pltpu.SMEM)
NT = (((1,), (1,)), ((), ()))
TN = (((0,), (0,)), ((), ()))


def halves(x):
    high = x.astype(jnp.bfloat16)
    return high, (x - high.astype(jnp.float32)).astype(jnp.bfloat16)


def stacked(x):
    return jnp.concatenate(halves(x), axis=0)


def apply_operator(left, own, right, hamiltonian, offsets, pairs):
    rows = own.shape[0]
    count, size, depth = hamiltonian.shape
    neighbours = depth // size
    line = stacked(jnp.concatenate([left, own, right], axis=1))
    blocks = line.shape[1] // size
    for tile in range(blocks // 2):
        pairs[2 * tile + 1] = line[:, tile * LANES : (tile + 1) * LANES]
    for tile in range(blocks // 2 + 1):
        lo, hi = tile * LANES - size, tile * LANES + size
        if lo < 0:
            part = jnp.concatenate([line[:, :size], line[:, :size]], axis=1)
        elif hi > line.shape[1]:
            part = jnp.concatenate([line[:, lo:], line[:, lo:]], axis=1)
        else:
            part = line[:, lo:hi]
        pairs[2 * tile] = part
    low_lanes = lax.broadcasted_iota(jnp.int32, (2 * rows, LANES), 1) < size
    results = []
    for b in range(count):
        picked = []
        for k in range(0, neighbours - 1, 2):
            first = pairs[b + REACH + offsets[b, k] + 1]
            second = pairs[b + REACH + offsets[b, k + 1]]
            picked.append(jnp.where(low_lanes, first, second))
        whole = len(picked) * LANES
        total = lax.dot_general(
            jnp.concatenate(picked, axis=1),
            hamiltonian[b, :, :whole],
            NT,
            preferred_element_type=jnp.float32,
        )
        if neighbours % 2:
            last = pairs[b + REACH + offsets[b, neighbours - 1] + 1][:, :size]
            total += lax.dot_general(
                last, hamiltonian[b, :, whole:], NT, preferred_element_type=jnp.float32
            )
        results.append(total[:rows] + total[rows:])
    return jnp.concatenate(results, axis=1)


def first_kernel(left, own, right, hamiltonian, offsets, center, width, out, head, tail, pairs):
    rim = head.shape[1]
    field = own[...]
    applied = apply_operator(left[:, -rim:], field, right[:, :rim], hamiltonian, offsets, pairs)
    first = (applied - center[0] * field) / width[0]
    out[...] = first
    head[...] = first[:, :rim]
    tail[...] = first[:, -rim:]


def second_kernel(left, own, right, hamiltonian, offsets, center, width, before, out, pairs):
    field = own[...]
    applied = apply_operator(left[...], field, right[...], hamiltonian, offsets, pairs)
    out[...] = 2.0 * (applied - center[0] * field) / width[0] - before[...]


def gram_kernel(total_nodes, *refs):
    parts, (gathered, gram) = refs[:-2], refs[-2:]
    count = len(parts)
    rows = parts[0].shape[0]
    me = lax.axis_index("states")
    for step, part in enumerate(parts):
        place = lax.rem(me + count - step, count)
        high, low = halves(part[...])
        gathered[0, pl.ds(pl.multiple_of(place * rows, rows), rows)] = high
        gathered[1, pl.ds(pl.multiple_of(place * rows, rows), rows)] = low
    states = count * rows
    both = gathered[...].reshape(2 * states, -1)
    terms = lax.dot_general(both, both, NT, preferred_element_type=jnp.float32)
    gram[...] = (terms[:states, :states] + (terms[:states, states:] + terms[states:, :states])) * (
        1.0 / total_nodes
    )


def inverse_factor(matrix, inverse):
    order = matrix.shape[0]
    lane = lax.broadcasted_iota(jnp.int32, (PANEL, order), 1)
    row = lax.broadcasted_iota(jnp.int32, (PANEL, order), 0)
    for start in range(0, order, PANEL):
        stop = start + PANEL
        panel = matrix[start:stop]
        inside = (lane >= start) & (lane < stop)
        columns = [
            jnp.broadcast_to(panel[:, start + k : start + k + 1], (PANEL, order))
            for k in range(PANEL)
        ]
        rows = jnp.where(inside, jnp.where(lane == row + start, 1.0, 0.0), panel)
        for j in range(PANEL):
            scale = lax.rsqrt(columns[j][j : j + 1])
            factor = columns[j] * scale
            pivot = rows[j : j + 1] * scale
            rows = jnp.where(row > j, rows - factor * pivot, jnp.where(row == j, pivot, rows))
            for k in range(j + 1, PANEL):
                columns[k] = columns[k] - factor * (columns[k][j : j + 1] * scale)
        inverse[start:stop] = jnp.where(lane < stop, rows, 0.0)
        if stop < order:
            beyond = jnp.where(lane >= stop, rows, 0.0)
            update = lax.dot_general(
                beyond, rows, TN, precision=lax.Precision.HIGHEST, preferred_element_type=jnp.float32
            )
            rest = matrix[stop:]
            rest_lane = lax.broadcasted_iota(jnp.int32, rest.shape, 1)
            kept = jnp.where((rest_lane >= start) & (rest_lane < stop), 0.0, rest)
            matrix[stop:] = kept - update[stop:]


def rotate_kernel(grams, gathered, out, matrix, inverse):
    total = grams[0]
    for i in range(1, grams.shape[0]):
        total += grams[i]
    matrix[...] = total
    inverse_factor(matrix, inverse)
    rows = out.shape[0]
    me = lax.axis_index("states")
    high, low = halves(inverse[pl.ds(pl.multiple_of(me * rows, rows), rows)])
    both = lax.dot_general(
        jnp.concatenate([high, low], axis=0),
        gathered[0],
        (((1,), (0,)), ((), ())),
        preferred_element_type=jnp.float32,
    )
    rest = jnp.dot(high, gathered[1], preferred_element_type=jnp.float32)
    out[...] = both[:rows] + (both[rows:] + rest)


def on_device(states_block, hamiltonian, offsets, center, halfwidth):
    rows, local = states_block.shape
    count, size, depth = hamiltonian.shape
    rim = REACH * size
    ring = lax.axis_size("nodes")
    parts = lax.axis_size("states")
    states = rows * parts
    up = [(i, (i + 1) % ring) for i in range(ring)]
    down = [((i + 1) % ring, i) for i in range(ring)]
    f32 = jnp.float32

    def shape(*dims, dtype=f32):
        return jax.ShapeDtypeStruct(dims, dtype)

    pairs = pltpu.VMEM((count + 2 * REACH + 1, 2 * rows, LANES), jnp.bfloat16)
    from_left = lax.ppermute(states_block, "nodes", up)
    from_right = lax.ppermute(states_block, "nodes", down)
    first, head, tail = pl.pallas_call(
        first_kernel,
        out_shape=(shape(rows, local), shape(rows, rim), shape(rows, rim)),
        in_specs=[VMEM] * 4 + [SMEM] * 3,
        out_specs=(VMEM,) * 3,
        scratch_shapes=[pairs],
        name="first",
    )(from_left, states_block, from_right, hamiltonian, offsets, center, halfwidth)
    from_left = lax.ppermute(tail, "nodes", up)
    from_right = lax.ppermute(head, "nodes", down)
    second = pl.pallas_call(
        second_kernel,
        out_shape=shape(rows, local),
        in_specs=[VMEM] * 4 + [SMEM] * 3 + [VMEM],
        out_specs=VMEM,
        scratch_shapes=[pairs],
        name="second",
    )(from_left, first, from_right, hamiltonian, offsets, center, halfwidth, states_block)
    gathering = [second] + [
        lax.ppermute(second, "states", [(i, (i + k) % parts) for i in range(parts)])
        for k in range(1, parts)
    ]
    gathered, gram = pl.pallas_call(
        functools.partial(gram_kernel, local * ring),
        out_shape=(shape(2, states, local, dtype=jnp.bfloat16), shape(states, states)),
        in_specs=[VMEM] * parts,
        out_specs=(VMEM, VMEM),
        name="gram",
    )(*gathering)
    if ring <= 16:
        grams = lax.all_gather(gram, "nodes")
    else:
        grams = lax.psum(gram, "nodes")[None]
    return pl.pallas_call(
        rotate_kernel,
        out_shape=shape(rows, local),
        in_specs=[VMEM] * 2,
        out_specs=VMEM,
        scratch_shapes=[pltpu.VMEM((states, states), f32)] * 2,
        name="rotate",
    )(grams, gathered)


def solution(mesh):
    placed = (P("states", "nodes"), P("nodes", None, None), P("nodes", None), P(), P())
    return jax.shard_map(
        on_device, mesh=mesh, in_specs=placed, out_specs=P("states", "nodes"), check_vma=False
    )
```

time: 155 us -> 49.6 us (0.32)
  waiting for transfers between devices: 55.2 us -> 10.7 us
  local copies, waits for them, and re-layouts: 28.6 us -> 1.86 us
  other arithmetic: 26.2 us -> 0 us
  Pallas kernels: 0 us -> 14 us
  between operations: 14.8 us -> 1.32 us
  matrix products: 8.27 us -> 0 us
  starting transfers between devices: 6.09 us -> 10.6 us
  blocking collectives: 14.9 us -> 10.8 us
    psum x1 -> x0, waiting for transfers between devices: 53.6 us -> none  [on_device(): intersection = lax.psum(terms, 'nodes') / total_nodes]
    another operation x5 -> x0, other arithmetic: 22.9 us -> none  [the longest x3 12.4 us: on_device(): lower = jnp.linalg.cholesky(intersection)]
    reshape x10 -> x0, local copies, waits for them, and re-layouts: 21.8 us -> none  [the longest x4 21.3 us: apply_local(): blocked[:, index].reshape(local_states, count, hamiltonian.shape[2])]
    pallas_call x0 -> x4, Pallas kernels: none -> 14 us  [the longest x1 5.87 us: on_device(): pl.pallas_call(rotate_kernel, out_shape=shape(rows, local), in_specs=[VME...]
    ppermute x4 -> x7, waiting for transfers between devices: 1.6 us -> 10.7 us  [the longest x3 5.26 us: on_device(): lax.ppermute(second, 'states', [(i, (i + k) % parts) for i in range(parts)])]
    dot_general x4 -> x0, matrix products: 8.02 us -> none  [the longest x2 6.11 us: apply_local(): jnp.einsum('bim,cbm->cbi', hamiltonian.astype(jnp.float32), picked, preci...]
    gather x2 -> x0, local copies, waits for them, and re-layouts: 5.52 us -> none  [apply_local(): blocked[:, index].reshape(local_states, count, hamiltonian.shape[2])]
    ppermute x4 -> x7, starting transfers between devices: 6.09 us -> 10.6 us  [the longest x3 4.61 us: on_device(): lax.ppermute(second, 'states', [(i, (i + k) % parts) for i in range(parts)])]
  transfers between devices with their start and end apart: 5 -> 7, of which waited for: 2 -> 6; matrix products, arithmetic and copies ran while one was open for 1% -> 0% of each run, Pallas kernels for 0% -> 0%
where the time goes in v1:
time: 49.6 us; the launch traced here: 49.2 us
  Pallas kernels  14 us (28%)
  blocking collectives  10.8 us (22%)
  waiting for transfers between devices  10.7 us (22%)
  starting transfers between devices  10.6 us (21%)
  local copies, waits for them, and re-layouts  1.86 us (4%)
  between operations  1.32 us (3%)
    all_gather x1, blocking collectives, on_device(): grams = lax.all_gather(gram, 'nodes')  10.8 us
    pallas_call x1, Pallas kernels, on_device(): pl.pallas_call(rotate_kernel, out_shape=shape(rows, local), in_specs=[VME...  5.87 us
    ppermute x3, waiting for transfers between devices, on_device(): lax.ppermute(second, 'states', [(i, (i + k) % parts) for i in range(parts)])  5.26 us
    ppermute x3, starting transfers between devices, on_device(): lax.ppermute(second, 'states', [(i, (i + k) % parts) for i in range(parts)])  4.61 us
    ppermute x1, starting transfers between devices, on_device(): from_right = lax.ppermute(states_block, 'nodes', down)  3.33 us
    pallas_call x1, Pallas kernels, on_device(): pl.pallas_call(first_kernel, out_shape=(shape(rows, local), shape(rows, r...  3.16 us
    pallas_call x1, Pallas kernels, on_device(): pl.pallas_call(second_kernel, out_shape=shape(rows, local), in_specs=[VME...  3.08 us
    ppermute x1, starting transfers between devices, on_device(): from_right = lax.ppermute(head, 'nodes', down)  2.64 us
  transfers between devices with their start and end apart: 7, of which 6 were waited for; matrix products, arithmetic and copies ran while one was open for 0% of the time, Pallas kernels for 0%

profile of v1, /device:TPU:0, one launch (start us, length us, event | category | flops | bytes accessed | tf_op | source)
XLA Modules:
  0.0 49.2 jit_solution(3632105743892512280)
XLA Ops:
  0.0 3.3 %collective-permute-start.1 = (f32[32,512]{1,0:T(8,128)}, f32[32,512]{1,0:T(8,128)S(1)}, u32[]{:S(2)}, u32[]{:S(2)}) collective-permute-start(f32[32,512]{1,0:T(8,128)} %before.1), channel_id=1, source_target_pairs={{4,0},{8,4},{12,8},{16,12},{20,16},{24,20},{28,24},{0,28},{5,1},{9... | collective-permute-start | bytes 196616 | tf_op jit(solution)/shard_map/ppermute | solution.py:170
  3.3 0.0 collective-permute-start
  4.6 0.9 %collective-permute-done.1.right = f32[32,512]{1,0:T(8,128)S(1)} collective-permute-done((f32[32,512]{1,0:T(8,128)}, f32[32,512]{1,0:T(8,128)S(1)}, u32[]{:S(2)}, u32[]{:S(2)}) %collective-permute-start.1) | collective-permute-done | bytes 65568 | tf_op jit(solution)/shard_map/ppermute | solution.py:170
  5.6 2.6 %collective-permute-done.left = f32[32,512]{1,0:T(8,128)S(1)} collective-permute-done((f32[32,512]{1,0:T(8,128)}, f32[32,512]{1,0:T(8,128)S(1)}, u32[]{:S(2)}, u32[]{:S(2)}) %collective-permute-start) | collective-permute-done | bytes 65568 | tf_op jit(solution)/shard_map/ppermute | solution.py:169
  8.1 0.0 copy-done
  8.1 0.6 %copy-done.1 = f32[32,512]{1,0:T(8,128)} copy-done((f32[32,512]{1,0:T(8,128)}, f32[32,512]{1,0:T(8,128)S(1)}, u32[]{:S(2)}) %copy-start.1) | copy-done | bytes 65560
  8.8 3.2 %first.1 = (f32[32,512]{1,0:T(8,128)}, f32[32,256]{1,0:T(8,128)}, f32[32,256]{1,0:T(8,128)}) custom-call(f32[32,512]{1,0:T(8,128)} %copy-done.1, f32[32,512]{1,0:T(8,128)} %before.1, f32[32,512]{1,0:T(8,128)} %copy-done, bf16[8,64,1728]{2,1,0:T(8,128)(2,1)} %hamiltonian.3, s32[8,27]{1,0:T(8,128)} %offsets.3, f32[1]{0:T(128)S(6)} %copy.6.center, f32[1]{0:T(128)S(6)} %copy.7.width), custom_call_target="tpu_custom_call" | custom-call | tf_op jit(solution)/shard_map/first/pallas_call | solution.py:171
  11.9 0.0 collective-permute-start.2
  11.9 2.6 %collective-permute-start.3 = (f32[32,256]{1,0:T(8,128)}, f32[32,256]{1,0:T(8,128)S(1)}, u32[]{:S(2)}, u32[]{:S(2)}) collective-permute-start(f32[32,256]{1,0:T(8,128)} %get-tuple-element.12), channel_id=1, source_target_pairs={{4,0},{8,4},{12,8},{16,12},{20,16},{24,20},{28,24},{0,28},{5,1},{9... | collective-permute-start | bytes 98312 | tf_op jit(solution)/shard_map/ppermute | solution.py:180
  14.6 1.9 %collective-permute-done.2.left = f32[32,256]{1,0:T(8,128)S(1)} collective-permute-done((f32[32,256]{1,0:T(8,128)}, f32[32,256]{1,0:T(8,128)S(1)}, u32[]{:S(2)}, u32[]{:S(2)}) %collective-permute-start.2) | collective-permute-done | bytes 32800 | tf_op jit(solution)/shard_map/ppermute | solution.py:179
  16.4 0.0 collective-permute-done.3.right
  16.5 0.6 %copy-done.5 = f32[32,256]{1,0:T(8,128)} copy-done((f32[32,256]{1,0:T(8,128)}, f32[32,256]{1,0:T(8,128)S(1)}, u32[]{:S(2)}) %copy-start.5) | copy-done | bytes 32792
  17.1 0.0 copy-done.6
  17.1 3.1 %second.1.refs_0_ = f32[32,512]{1,0:T(8,128)} custom-call(f32[32,256]{1,0:T(8,128)} %copy-done.5, f32[32,512]{1,0:T(8,128)} %get-tuple-element.11.own, f32[32,256]{1,0:T(8,128)} %copy-done.6, bf16[8,64,1728]{2,1,0:T(8,128)(2,1)} %hamiltonian.3, s32[8,27]{1,0:T(8,128)} %offsets.3, f32[1]{0:T(128)S(6)} %copy.6.center, f32[1]{0:T(128)S(6)} %copy.7.width, ...), custom_call_target="tpu_custom_call" | custom-call | tf_op jit(solution)/shard_map/second/pallas_call | solution.py:181
  20.2 3.6 %collective-permute-start.6 = (f32[32,512]{1,0:T(8,128)}, f32[32,512]{1,0:T(8,128)S(1)}, u32[]{:S(2)}, u32[]{:S(2)}) collective-permute-start(f32[32,512]{1,0:T(8,128)} %second.1.refs_0_), channel_id=1, source_target_pairs={{0,3},{1,0},{2,1},{3,2},{4,7},{5,4},{6,5},{7,6},{8,11},{9,8},{10,9... | collective-permute-start | bytes 196616 | tf_op jit(solution)/shard_map/ppermute | solution.py:190
  23.8 0.0 collective-permute-start.5
  23.8 1.0 %collective-permute-start.4 = (f32[32,512]{1,0:T(8,128)}, f32[32,512]{1,0:T(8,128)S(1)}, u32[]{:S(2)}, u32[]{:S(2)}) collective-permute-start(f32[32,512]{1,0:T(8,128)} %second.1.refs_0_), channel_id=1, source_target_pairs={{0,1},{1,2},{2,3},{3,0},{4,5},{5,6},{6,7},{7,4},{8,9},{9,10},{10,1... | collective-permute-start | bytes 196616 | tf_op jit(solution)/shard_map/ppermute | solution.py:190
  24.8 1.2 %collective-permute-done.6.refs_3_ = f32[32,512]{1,0:T(8,128)S(1)} collective-permute-done((f32[32,512]{1,0:T(8,128)}, f32[32,512]{1,0:T(8,128)S(1)}, u32[]{:S(2)}, u32[]{:S(2)}) %collective-permute-start.6) | collective-permute-done | bytes 65568 | tf_op jit(solution)/shard_map/ppermute | solution.py:190
  26.0 3.2 %collective-permute-done.5.refs_2_ = f32[32,512]{1,0:T(8,128)S(1)} collective-permute-done((f32[32,512]{1,0:T(8,128)}, f32[32,512]{1,0:T(8,128)S(1)}, u32[]{:S(2)}, u32[]{:S(2)}) %collective-permute-start.5) | collective-permute-done | bytes 65568 | tf_op jit(solution)/shard_map/ppermute | solution.py:190
  29.1 0.9 %collective-permute-done.4.refs_1_ = f32[32,512]{1,0:T(8,128)S(1)} collective-permute-done((f32[32,512]{1,0:T(8,128)}, f32[32,512]{1,0:T(8,128)S(1)}, u32[]{:S(2)}, u32[]{:S(2)}) %collective-permute-start.4) | collective-permute-done | bytes 65568 | tf_op jit(solution)/shard_map/ppermute | solution.py:190
  30.1 0.6 %copy-done.4 = f32[32,512]{1,0:T(8,128)} copy-done((f32[32,512]{1,0:T(8,128)}, f32[32,512]{1,0:T(8,128)S(1)}, u32[]{:S(2)}) %copy-start.4) | copy-done | bytes 65560
  30.7 1.8 %gram.1 = (bf16[2,128,512]{2,1,0:T(8,128)(2,1)}, f32[128,128]{1,0:T(8,128)}) custom-call(f32[32,512]{1,0:T(8,128)} %second.1.refs_0_, f32[32,512]{1,0:T(8,128)} %copy-done.4, f32[32,512]{1,0:T(8,128)} %copy-done.3, f32[32,512]{1,0:T(8,128)} %copy-done.2), custom_call_target="tpu_custom_call" | custom-call | tf_op jit(solution)/shard_map/gram/pallas_call | solution.py:193
  32.5 10.8 %all-gather = f32[1024,128]{1,0:T(8,128)} all-gather(f32[128,128]{1,0:T(8,128)} %get-tuple-element.13), channel_id=2, replica_groups=mesh['nodes'=8,'states'=4] {'nodes'}, dimensions={0}, use_global_device_ids=true | all-gather | bytes 589824 | tf_op jit(solution)/shard_map/all_gather | solution.py:201
  43.4 5.9 %rotate.1 = f32[32,512]{1,0:T(8,128)} custom-call(f32[8,128,128]{2,1,0:T(8,128)} %bitcast.1, bf16[2,128,512]{2,1,0:T(8,128)(2,1)} %get-tuple-element.14.gathered), custom_call_target="tpu_custom_call" | custom-call | tf_op jit(solution)/shard_map/rotate/pallas_call | solution.py:204
  (9 shorter events, 0.0 us)
Async XLA Ops:
  0.0 5.6 %collective-permute-start.1 = (f32[32,512]{1,0:T(8,128)}, f32[32,512]{1,0:T(8,128)S(1)}, u32[]{:S(2)}, u32[]{:S(2)}) collective-permute-start(f32[32,512]{1,0:T(8,128)} %before.1), channel_id=1, source_target_pairs={{4,0},{8,4},{12,8},{16,12},{20,16},{24,20},{28,24},{0,28},{5,1},{9... | collective-permute-start | bytes 196616 | tf_op jit(solution)/shard_map/ppermute | solution.py:170
  3.3 4.8 %collective-permute-start = (f32[32,512]{1,0:T(8,128)}, f32[32,512]{1,0:T(8,128)S(1)}, u32[]{:S(2)}, u32[]{:S(2)}) collective-permute-start(f32[32,512]{1,0:T(8,128)} %before.1), channel_id=1, source_target_pairs={{0,4},{4,8},{8,12},{12,16},{16,20},{20,24},{24,28},{28,0},{1,5},{5... | collective-permute-start | bytes 196616 | tf_op jit(solution)/shard_map/ppermute | solution.py:169
  5.6 2.6 %copy-start = (f32[32,512]{1,0:T(8,128)}, f32[32,512]{1,0:T(8,128)S(1)}, u32[]{:S(2)}) copy-start(f32[32,512]{1,0:T(8,128)S(1)} %collective-permute-done.1.right) | copy-start | bytes 196612
  8.1 0.6 %copy-start.1 = (f32[32,512]{1,0:T(8,128)}, f32[32,512]{1,0:T(8,128)S(1)}, u32[]{:S(2)}) copy-start(f32[32,512]{1,0:T(8,128)S(1)} %collective-permute-done.left) | copy-start | bytes 196612
  11.9 4.5 %collective-permute-start.2 = (f32[32,256]{1,0:T(8,128)}, f32[32,256]{1,0:T(8,128)S(1)}, u32[]{:S(2)}, u32[]{:S(2)}) collective-permute-start(f32[32,256]{1,0:T(8,128)} %get-tuple-element.10), channel_id=1, source_target_pairs={{0,4},{4,8},{8,12},{12,16},{16,20},{20,24},{24,28},{28,0},{1,5},{5... | collective-permute-start | bytes 98312 | tf_op jit(solution)/shard_map/ppermute | solution.py:179
  11.9 4.6 %collective-permute-start.3 = (f32[32,256]{1,0:T(8,128)}, f32[32,256]{1,0:T(8,128)S(1)}, u32[]{:S(2)}, u32[]{:S(2)}) collective-permute-start(f32[32,256]{1,0:T(8,128)} %get-tuple-element.12), channel_id=1, source_target_pairs={{4,0},{8,4},{12,8},{16,12},{20,16},{24,20},{28,24},{0,28},{5,1},{9... | collective-permute-start | bytes 98312 | tf_op jit(solution)/shard_map/ppermute | solution.py:180
  16.4 0.6 %copy-start.5 = (f32[32,256]{1,0:T(8,128)}, f32[32,256]{1,0:T(8,128)S(1)}, u32[]{:S(2)}) copy-start(f32[32,256]{1,0:T(8,128)S(1)} %collective-permute-done.2.left) | copy-start | bytes 98308
  16.5 0.6 %copy-start.6 = (f32[32,256]{1,0:T(8,128)}, f32[32,256]{1,0:T(8,128)S(1)}, u32[]{:S(2)}) copy-start(f32[32,256]{1,0:T(8,128)S(1)} %collective-permute-done.3.right) | copy-start | bytes 98308
  20.2 5.8 %collective-permute-start.6 = (f32[32,512]{1,0:T(8,128)}, f32[32,512]{1,0:T(8,128)S(1)}, u32[]{:S(2)}, u32[]{:S(2)}) collective-permute-start(f32[32,512]{1,0:T(8,128)} %second.1.refs_0_), channel_id=1, source_target_pairs={{0,3},{1,0},{2,1},{3,2},{4,7},{5,4},{6,5},{7,6},{8,11},{9,8},{10,9... | collective-permute-start | bytes 196616 | tf_op jit(solution)/shard_map/ppermute | solution.py:190
  23.8 5.4 %collective-permute-start.5 = (f32[32,512]{1,0:T(8,128)}, f32[32,512]{1,0:T(8,128)S(1)}, u32[]{:S(2)}, u32[]{:S(2)}) collective-permute-start(f32[32,512]{1,0:T(8,128)} %second.1.refs_0_), channel_id=1, source_target_pairs={{0,2},{1,3},{2,0},{3,1},{4,6},{5,7},{6,4},{7,5},{8,10},{9,11},{10,... | collective-permute-start | bytes 196616 | tf_op jit(solution)/shard_map/ppermute | solution.py:190
  23.8 6.3 %collective-permute-start.4 = (f32[32,512]{1,0:T(8,128)}, f32[32,512]{1,0:T(8,128)S(1)}, u32[]{:S(2)}, u32[]{:S(2)}) collective-permute-start(f32[32,512]{1,0:T(8,128)} %second.1.refs_0_), channel_id=1, source_target_pairs={{0,1},{1,2},{2,3},{3,0},{4,5},{5,6},{6,7},{7,4},{8,9},{9,10},{10,1... | collective-permute-start | bytes 196616 | tf_op jit(solution)/shard_map/ppermute | solution.py:190
  26.0 4.1 %copy-start.2 = (f32[32,512]{1,0:T(8,128)}, f32[32,512]{1,0:T(8,128)S(1)}, u32[]{:S(2)}) copy-start(f32[32,512]{1,0:T(8,128)S(1)} %collective-permute-done.6.refs_3_) | copy-start | bytes 196612
  29.1 0.9 %copy-start.3 = (f32[32,512]{1,0:T(8,128)}, f32[32,512]{1,0:T(8,128)S(1)}, u32[]{:S(2)}) copy-start(f32[32,512]{1,0:T(8,128)S(1)} %collective-permute-done.5.refs_2_) | copy-start | bytes 196612
  30.1 0.6 %copy-start.4 = (f32[32,512]{1,0:T(8,128)}, f32[32,512]{1,0:T(8,128)S(1)}, u32[]{:S(2)}) copy-start(f32[32,512]{1,0:T(8,128)S(1)} %collective-permute-done.4.refs_1_) | copy-start | bytes 196612

commit v2 on v1

v2 whole, which is shorter than its diff:
```python
import functools

import jax
import jax.numpy as jnp
from jax import lax
from jax.experimental import pallas as pl
from jax.experimental.pallas import tpu as pltpu
from jax.sharding import PartitionSpec as P

REACH = 4
LANES = 128
PANEL = 16
VMEM = pl.BlockSpec(memory_space=pltpu.VMEM)
SMEM = pl.BlockSpec(memory_space=pltpu.SMEM)
HBM = pl.BlockSpec(memory_space=pltpu.HBM)
ROOM = pltpu.CompilerParams(vmem_limit_bytes=16 * 2**20)
NT = (((1,), (1,)), ((), ()))
TN = (((0,), (0,)), ((), ()))


def halves(x):
    high = x.astype(jnp.bfloat16)
    return high, (x - high.astype(jnp.float32)).astype(jnp.bfloat16)


def stacked(x):
    return jnp.concatenate(halves(x), axis=0)


def swapped(tile):
    half = LANES // 2
    return jnp.concatenate([tile[:, half:], tile[:, :half]], axis=1)


def prepare(there, offsets_there, *refs):
    near_band, far_band, matrix, near_sums, far_sums, offsets, sems = refs
    odd = lax.axis_index("nodes") % 2 == 1
    count, size, depth = matrix.shape
    neighbours = depth // size
    span = 2 * REACH + 1
    begin = jnp.where(odd, 0, count - REACH)

    def copy(b):
        return pltpu.make_async_copy(there.at[b], matrix.at[b], sems.at[b])

    distances = pltpu.make_async_copy(offsets_there, offsets, sems.at[count])
    distances.start()
    rows = [lax.rem(begin + r, count) for r in range(count)]
    for b in rows:
        copy(b).start()
    low_lanes = lax.broadcasted_iota(jnp.int32, (size, LANES), 1) < size
    for sums in (near_sums, far_sums):
        sums[...] = jnp.zeros(sums.shape, jnp.float32)
    distances.wait()
    for sums, band, mine in ((near_sums, near_band, rows[:REACH]), (far_sums, far_band, rows[REACH:])):
        for b in mine:
            copy(b).wait()
        for k in range(0, neighbours, 2):
            for r, b in enumerate(mine):
                tile = matrix[b, :, k * size : min(k + 2, neighbours) * size].astype(jnp.float32)
                if tile.shape[1] < LANES:
                    tile = jnp.concatenate([tile, jnp.zeros_like(tile)], axis=1)
                for j in range(k, min(k + 2, neighbours)):
                    place = offsets[b, j] + REACH
                    sums[r, j - k, place] = sums[r, j - k, place] + tile
        for r in range(REACH):
            for t in range(3 * REACH // 2):
                low, high = 2 * t - r, 2 * t + 1 - r
                zero = jnp.zeros((size, LANES), jnp.float32)
                even_low, odd_low = (
                    (sums[r, 0, low], sums[r, 1, low]) if 0 <= low < span else (zero, zero)
                )
                even_high, odd_high = (
                    (sums[r, 0, high], sums[r, 1, high]) if 0 <= high < span else (zero, zero)
                )
                whole = jnp.where(low_lanes, even_low, odd_high) + swapped(
                    jnp.where(low_lanes, even_high, odd_low)
                )
                top, rest = halves(whole)
                place = (slice(r * size, (r + 1) * size), slice(t * LANES, (t + 1) * LANES))
                band[(0, *place)] = top
                band[(1, *place)] = rest


def side(field, before):
    half = field.shape[1] // 2
    return jnp.where(before, field[:, :half], field[:, half:])


def joined(near, far, odd):
    return jnp.concatenate([jnp.where(odd, near, far), jnp.where(odd, far, near)], axis=1)


def before_own(is_near):
    odd = lax.axis_index("nodes") % 2
    return odd == (1 if is_near else 0)


def window(own, rim, before):
    wide = rim.shape[1]
    return jnp.concatenate(
        [
            jnp.where(before, rim, own[:, :wide]),
            jnp.where(before, own[:, :wide], own[:, wide:]),
            jnp.where(before, own[:, wide:], rim),
        ],
        axis=1,
    )


def apply_band(field, band):
    rows = field.shape[0]
    field = stacked(field)
    both = lax.dot_general(field, band[0], NT, preferred_element_type=jnp.float32)
    rest = lax.dot_general(field[:rows], band[1], NT, preferred_element_type=jnp.float32)
    return both[:rows] + (both[rows:] + rest)


def first_kernel(is_near, rim, own, band, out):
    before = before_own(is_near)
    out[...] = apply_band(window(own[...], side(rim[...], jnp.logical_not(before)), before), band)


def second_half(is_near, rim, near, far, band, earlier_rim, earlier, center, width):
    before = before_own(is_near)
    shift, scale = center[0], 1.0 / width[0]
    applied = window(joined(near[...], far[...], before_own(True)), rim[...], before)
    field = earlier[...]
    states = window(field, side(earlier_rim[...], jnp.logical_not(before)), before)
    first = (applied - shift * states) * scale
    half = rim.shape[1]
    mine = first[:, half : 2 * half]
    return 2.0 * ((apply_band(first, band) - shift * mine) * scale) - side(field, before)


def second_near(*refs):
    refs[-1][...] = second_half(True, *refs[:-1])


def second_far(*refs):
    *rest, done, out = refs
    out[...] = joined(done[...], second_half(False, *rest), before_own(True))


def gram_kernel(total_nodes, steps, *refs):
    parts, (gathered, gram) = refs[:-2], refs[-2:]
    rows = parts[0].shape[0]
    me = lax.axis_index("states")
    for step, part in zip(steps, parts, strict=True):
        place = pl.ds(pl.multiple_of((me ^ step) * rows, rows), rows)
        high, low = halves(part[...])
        gathered[0, place] = high
        gathered[1, place] = low
    states = len(parts) * rows
    both = gathered[...].reshape(2 * states, -1)
    terms = lax.dot_general(both, both, NT, preferred_element_type=jnp.float32)
    gram[...] = (terms[:states, :states] + (terms[:states, states:] + terms[states:, :states])) * (
        1.0 / total_nodes
    )


def sum_kernel(*refs):
    refs[-1][...] = functools.reduce(jnp.add, [ref[...] for ref in refs[:-1]])


def inverse_factor(matrix, inverse):
    order = matrix.shape[0]
    lane = lax.broadcasted_iota(jnp.int32, (PANEL, order), 1)
    row = lax.broadcasted_iota(jnp.int32, (PANEL, order), 0)
    for start in range(0, order, PANEL):
        stop = start + PANEL
        panel = matrix[start:stop]
        inside = (lane >= start) & (lane < stop)
        columns = [
            jnp.broadcast_to(panel[:, start + k : start + k + 1], (PANEL, order))
            for k in range(PANEL)
        ]
        rows = jnp.where(inside, jnp.where(lane == row + start, 1.0, 0.0), panel)
        for j in range(PANEL):
            scale = lax.rsqrt(columns[j][j : j + 1])
            factor = columns[j] * scale
            pivot = rows[j : j + 1] * scale
            rows = jnp.where(row > j, rows - factor * pivot, jnp.where(row == j, pivot, rows))
            for k in range(j + 1, PANEL):
                columns[k] = columns[k] - factor * (columns[k][j : j + 1] * scale)
        inverse[start:stop] = jnp.where(lane < stop, rows, 0.0)
        if stop < order:
            beyond = jnp.where(lane >= stop, rows, 0.0)
            update = lax.dot_general(
                beyond, rows, TN, precision=lax.Precision.HIGHEST, preferred_element_type=jnp.float32
            )
            rest = matrix[stop:]
            rest_lane = lax.broadcasted_iota(jnp.int32, rest.shape, 1)
            kept = jnp.where((rest_lane >= start) & (rest_lane < stop), 0.0, rest)
            matrix[stop:] = kept - update[stop:]


def rotate_kernel(*refs):
    *grams, gathered, out, matrix, inverse = refs
    matrix[...] = functools.reduce(jnp.add, [gram[...] for gram in grams])
    inverse_factor(matrix, inverse)
    rows = out.shape[0]
    me = lax.axis_index("states")
    high, low = halves(inverse[pl.ds(pl.multiple_of(me * rows, rows), rows)])
    both = lax.dot_general(
        jnp.concatenate([high, low], axis=0),
        gathered[0],
        (((1,), (0,)), ((), ())),
        preferred_element_type=jnp.float32,
    )
    rest = jnp.dot(high, gathered[1], preferred_element_type=jnp.float32)
    out[...] = both[:rows] + (both[rows:] + rest)


def near(x):
    return pltpu.with_memory_space_constraint(x, pltpu.VMEM)


def exchange(x, axis, step):
    count = lax.axis_size(axis)
    return near(lax.ppermute(x, axis, [(i, i ^ step) for i in range(count)]))


def on_device(states_block, hamiltonian, offsets, center, halfwidth):
    rows, local = states_block.shape
    count, size, depth = hamiltonian.shape
    half = local // 2
    ring = lax.axis_size("nodes")
    parts = lax.axis_size("states")
    states = rows * parts
    off_chip = [(i, (i + 1 if i % 2 else i - 1) % ring) for i in range(ring)]
    f32, bf16 = jnp.float32, jnp.bfloat16
    field = pltpu.VMEM((rows, local), f32)
    part = pltpu.VMEM((rows, half), f32)
    square = pltpu.VMEM((states, states), f32)
    band = pltpu.VMEM((2, REACH * size, 3 * REACH * size), bf16)
    sums = pltpu.VMEM((REACH, 2, 2 * REACH + 1, size, LANES), f32)

    def over_links(x):
        return near(lax.ppermute(x, "nodes", off_chip))

    def call(kernel, out, *operands, name):
        return near(
            pl.pallas_call(
                kernel,
                out_shape=out,
                in_specs=[SMEM if x.size == 1 else VMEM for x in operands],
                out_specs=VMEM,
                compiler_params=ROOM,
                name=name,
            )(*operands)
        )

    far_states = over_links(states_block)
    near_states = exchange(states_block, "nodes", 1)
    near_band, far_band = pl.pallas_call(
        prepare,
        out_shape=(band, band),
        in_specs=[HBM, HBM],
        out_specs=(VMEM, VMEM),
        scratch_shapes=[
            pltpu.VMEM(hamiltonian.shape, bf16),
            sums,
            sums,
            pltpu.SMEM(offsets.shape, jnp.int32),
            pltpu.SemaphoreType.DMA((count + 1,)),
        ],
        compiler_params=ROOM,
        name="prepare",
    )(*(pltpu.with_memory_space_constraint(x, pltpu.HBM) for x in (hamiltonian, offsets)))
    near_band, far_band = near(near_band), near(far_band)
    own = near(states_block)
    near_part = call(
        functools.partial(first_kernel, True), part, near_states, own, near_band, name="first_near"
    )
    near_rim = exchange(near_part, "nodes", 1)
    far_part = call(
        functools.partial(first_kernel, False), part, far_states, own, far_band, name="first_far"
    )
    far_rim = over_links(far_part)
    parts_of = (near_part, far_part)
    scalars = (center, halfwidth)
    near_second = call(
        second_near, part, near_rim, *parts_of, near_band, near_states, own, *scalars, name="second_near"
    )
    second = call(
        second_far,
        field,
        far_rim,
        *parts_of,
        far_band,
        far_states,
        own,
        *scalars,
        near_second,
        name="second_far",
    )
    steps = sorted(range(1, parts), key=lambda k: (k % 2, k))
    gathering = [second] + [exchange(second, "states", k) for k in steps]
    gathered, gram = pl.pallas_call(
        functools.partial(gram_kernel, local * ring, [0] + steps),
        out_shape=(pltpu.VMEM((2, states, local), bf16), square),
        in_specs=[VMEM] * parts,
        out_specs=(VMEM, VMEM),
        compiler_params=ROOM,
        name="gram",
    )(*gathering)
    terms = [near(gram), exchange(near(gram), "nodes", 1)]
    bit = 2
    while bit < ring:
        total = near(
            pl.pallas_call(
                sum_kernel,
                out_shape=square,
                in_specs=[VMEM] * len(terms),
                out_specs=VMEM,
                compiler_params=ROOM,
                name="sum",
            )(*terms)
        )
        peers = [bit, 2 * bit, 3 * bit] if 2 * bit < ring else [bit]
        terms = [total] + [exchange(total, "nodes", k) for k in peers]
        bit *= 4
    return pl.pallas_call(
        rotate_kernel,
        out_shape=jax.ShapeDtypeStruct((rows, local), f32),
        in_specs=[VMEM] * (len(terms) + 1),
        out_specs=VMEM,
        scratch_shapes=[square, square],
        compiler_params=ROOM,
        name="rotate",
    )(*terms, near(gathered))


def solution(mesh):
    placed = (P("states", "nodes"), P("nodes", None, None), P("nodes", None), P(), P())
    return jax.shard_map(
        on_device, mesh=mesh, in_specs=placed, out_specs=P("states", "nodes"), check_vma=False
    )
```

time: 49.6 us -> 35.5 us (0.72)
  blocking collectives: 10.8 us -> 0 us
  Pallas kernels: 14 us -> 9.59 us
  starting transfers between devices: 10.6 us -> 13.4 us
  local copies, waits for them, and re-layouts: 1.86 us -> 0.01 us
    all_gather x1 -> x0, blocking collectives: 10.8 us -> none  [on_device(): grams = lax.all_gather(gram, 'nodes')]
    pallas_call x4 -> x8, Pallas kernels: 14 us -> 9.59 us  [the longest x1 4.76 us: on_device(): pl.pallas_call(rotate_kernel, out_shape=jax.ShapeDtypeStruct((rows, local...]
    ppermute x7 -> x11, starting transfers between devices: 10.6 us -> 13.4 us  [the longest x9 8.6 us: exchange(): return near(lax.ppermute(x, axis, [(i, i ^ step) for i in range(count)]))]
    unnamed x14 -> x2, local copies, waits for them, and re-layouts: 1.86 us -> 0.01 us
    ppermute x7 -> x11, waiting for transfers between devices: 10.7 us -> 10.9 us  [the longest x9 9.46 us: exchange(): return near(lax.ppermute(x, axis, [(i, i ^ step) for i in range(count)]))]
  transfers between devices with their start and end apart: 7 -> 11, of which waited for: 6 -> 8; matrix products, arithmetic and copies ran while one was open for 0% -> 0% of each run, Pallas kernels for 0% -> 12%
where the time goes in v2:
time: 35.5 us; the launch traced here: 35.3 us
  starting transfers between devices  13.4 us (38%)
  waiting for transfers between devices  10.9 us (31%)
  Pallas kernels  9.59 us (27%)
  between operations  1.39 us (4%)
    ppermute x9, waiting for transfers between devices, exchange(): return near(lax.ppermute(x, axis, [(i, i ^ step) for i in range(count)]))  9.46 us
    ppermute x9, starting transfers between devices, exchange(): return near(lax.ppermute(x, axis, [(i, i ^ step) for i in range(count)]))  8.6 us
    ppermute x2, starting transfers between devices, over_links(): return near(lax.ppermute(x, 'nodes', off_chip))  4.82 us
    pallas_call x1, Pallas kernels, on_device(): pl.pallas_call(rotate_kernel, out_shape=jax.ShapeDtypeStruct((rows, local...  4.76 us
    pallas_call x1, Pallas kernels, on_device(): pl.pallas_call(prepare, out_shape=(band, band), in_specs=[HBM, HBM], out_...  3.15 us
    ppermute x2, waiting for transfers between devices, over_links(): return near(lax.ppermute(x, 'nodes', off_chip))  1.43 us
    pallas_call x4, Pallas kernels, call(): pl.pallas_call(kernel, out_shape=out, in_specs=[SMEM if x.size == 1 else...  1.37 us
  transfers between devices with their start and end apart: 11, of which 8 were waited for; matrix products, arithmetic and copies ran while one was open for 0% of the time, Pallas kernels for 12%

profile of v2, /device:TPU:0, one launch (start us, length us, event | category | flops | bytes accessed | tf_op | source)
XLA Modules:
  0.0 35.3 jit_solution(16383258494360924765)
XLA Ops:
  0.0 0.5 %collective-permute-start.2 = (f32[32,512]{1,0:T(8,128)}, f32[32,512]{1,0:T(8,128)S(1)}, u32[]{:S(2)}, u32[]{:S(2)}) collective-permute-start(f32[32,512]{1,0:T(8,128)} %refs_5_.3), channel_id=1, source_target_pairs={{0,4},{4,0},{8,12},{12,8},{16,20},{20,16},{24,28},{28,24},{1,5},{5... | collective-permute-start | bytes 196616 | tf_op jit(solution)/shard_map/ppermute | solution.py:221
  0.5 3.6 %collective-permute-start = (f32[32,512]{1,0:T(8,128)}, f32[32,512]{1,0:T(8,128)S(1)}, u32[]{:S(2)}, u32[]{:S(2)}) collective-permute-start(f32[32,512]{1,0:T(8,128)} %refs_5_.3), channel_id=1, source_target_pairs={{0,28},{4,8},{8,4},{12,16},{16,12},{20,24},{24,20},{28,0},{1,29},{... | collective-permute-start | bytes 196616 | tf_op jit(solution)/shard_map/ppermute | solution.py:240
  4.0 3.2 %prepare.1 = (bf16[2,256,768]{2,1,0:T(8,128)(2,1)S(1)}, bf16[2,256,768]{2,1,0:T(8,128)(2,1)S(1)}) custom-call(bf16[8,64,1728]{2,1,0:T(8,128)(2,1)} %there.1, s32[8,27]{1,0:T(8,128)} %offsets_there.1), custom_call_target="tpu_custom_call" | custom-call | tf_op jit(solution)/shard_map/prepare/pallas_call | solution.py:256
  7.2 0.3 first_near.1.refs_1_
  7.5 0.1 collective-permute-start.3
  7.6 0.3 first_far.1.refs_2_
  7.9 1.3 %collective-permute-start.1 = (f32[32,256]{1,0:T(8,128)S(1)}, f32[32,256]{1,0:T(8,128)S(1)}, u32[]{:S(2)}, u32[]{:S(2)}) collective-permute-start(f32[32,256]{1,0:T(8,128)S(1)} %first_far.1.refs_2_), channel_id=1, source_target_pairs={{0,28},{4,8},{8,4},{12,16},{16,12},{20,24},{24,20},{28,0},{1,29},{... | collective-permute-start | bytes 98312 | tf_op jit(solution)/shard_map/ppermute | solution.py:240
  10.5 0.4 %second_near.1.refs_8_ = f32[32,256]{1,0:T(8,128)S(1)} custom-call(f32[32,256]{1,0:T(8,128)S(1)} %collective-permute-done.3.refs_0_, f32[32,256]{1,0:T(8,128)S(1)} %first_near.1.refs_1_, f32[32,256]{1,0:T(8,128)S(1)} %first_far.1.refs_2_, bf16[2,256,768]{2,1,0:T(8,128)(2,1)S(1)} %get-tuple-element.10.band.refs_3_, ...), custom_call_target="tpu_custom_call" | custom-call | tf_op jit(solution)/shard_map/second_near/pallas_call | solution.py:244
  10.9 1.4 %collective-permute-done.1.refs_0_ = f32[32,256]{1,0:T(8,128)S(1)} collective-permute-done((f32[32,256]{1,0:T(8,128)S(1)}, f32[32,256]{1,0:T(8,128)S(1)}, u32[]{:S(2)}, u32[]{:S(2)}) %collective-permute-start.1) | collective-permute-done | bytes 32800 | tf_op jit(solution)/shard_map/ppermute | solution.py:240
  12.3 0.4 %second_far.1.refs_0_ = f32[32,512]{1,0:T(8,128)S(1)} custom-call(f32[32,256]{1,0:T(8,128)S(1)} %collective-permute-done.1.refs_0_, f32[32,256]{1,0:T(8,128)S(1)} %first_near.1.refs_1_, f32[32,256]{1,0:T(8,128)S(1)} %first_far.1.refs_2_, bf16[2,256,768]{2,1,0:T(8,128)(2,1)S(1)} %get-tuple-element.9.band.refs_3_, ...), custom_call_target="tpu_custom_call" | custom-call | tf_op jit(solution)/shard_map/second_far/pallas_call | solution.py:244
  12.7 3.7 %collective-permute-start.6 = (f32[32,512]{1,0:T(8,128)S(1)}, f32[32,512]{1,0:T(8,128)S(1)}, u32[]{:S(2)}, u32[]{:S(2)}) collective-permute-start(f32[32,512]{1,0:T(8,128)S(1)} %second_far.1.refs_0_), channel_id=1, source_target_pairs={{0,3},{1,2},{2,1},{3,0},{4,7},{5,6},{6,5},{7,4},{8,11},{9,10},{10,... | collective-permute-start | bytes 196616 | tf_op jit(solution)/shard_map/ppermute | solution.py:221
  16.3 0.8 %collective-permute-start.4 = (f32[32,512]{1,0:T(8,128)S(1)}, f32[32,512]{1,0:T(8,128)S(1)}, u32[]{:S(2)}, u32[]{:S(2)}) collective-permute-start(f32[32,512]{1,0:T(8,128)S(1)} %second_far.1.refs_0_), channel_id=1, source_target_pairs={{0,2},{1,3},{2,0},{3,1},{4,6},{5,7},{6,4},{7,5},{8,10},{9,11},{10,... | collective-permute-start | bytes 196616 | tf_op jit(solution)/shard_map/ppermute | solution.py:221
  17.1 2.1 %collective-permute-done.6.refs_3_ = f32[32,512]{1,0:T(8,128)S(1)} collective-permute-done((f32[32,512]{1,0:T(8,128)S(1)}, f32[32,512]{1,0:T(8,128)S(1)}, u32[]{:S(2)}, u32[]{:S(2)}) %collective-permute-start.6) | collective-permute-done | bytes 65568 | tf_op jit(solution)/shard_map/ppermute | solution.py:221
  19.2 1.9 %collective-permute-done.5.refs_2_ = f32[32,512]{1,0:T(8,128)S(1)} collective-permute-done((f32[32,512]{1,0:T(8,128)S(1)}, f32[32,512]{1,0:T(8,128)S(1)}, u32[]{:S(2)}, u32[]{:S(2)}) %collective-permute-start.5) | collective-permute-done | bytes 65568 | tf_op jit(solution)/shard_map/ppermute | solution.py:221
  21.1 0.8 %collective-permute-done.4.refs_1_ = f32[32,512]{1,0:T(8,128)S(1)} collective-permute-done((f32[32,512]{1,0:T(8,128)S(1)}, f32[32,512]{1,0:T(8,128)S(1)}, u32[]{:S(2)}, u32[]{:S(2)}) %collective-permute-start.4) | collective-permute-done | bytes 65568 | tf_op jit(solution)/shard_map/ppermute | solution.py:221
  22.0 0.3 gram.1
  22.3 1.2 %collective-permute-done.7.refs_1_ = f32[128,128]{1,0:T(8,128)S(1)} collective-permute-done((f32[128,128]{1,0:T(8,128)S(1)}, f32[128,128]{1,0:T(8,128)S(1)}, u32[]{:S(2)}, u32[]{:S(2)}) %collective-permute-start.7) | collective-permute-done | bytes 65568 | tf_op jit(solution)/shard_map/ppermute | solution.py:221
  23.6 0.3 collective-permute-start.10
  23.9 2.3 %collective-permute-start.9 = (f32[128,128]{1,0:T(8,128)S(1)}, f32[128,128]{1,0:T(8,128)S(1)}, u32[]{:S(2)}, u32[]{:S(2)}) collective-permute-start(f32[128,128]{1,0:T(8,128)S(1)} %sum.1.refs_0_), channel_id=1, source_target_pairs={{0,16},{4,20},{8,24},{12,28},{16,0},{20,4},{24,8},{28,12},{1,17},{... | collective-permute-start | bytes 196616 | tf_op jit(solution)/shard_map/ppermute | solution.py:221
  26.3 0.9 %collective-permute-start.8 = (f32[128,128]{1,0:T(8,128)S(1)}, f32[128,128]{1,0:T(8,128)S(1)}, u32[]{:S(2)}, u32[]{:S(2)}) collective-permute-start(f32[128,128]{1,0:T(8,128)S(1)} %sum.1.refs_0_), channel_id=1, source_target_pairs={{0,8},{4,12},{8,0},{12,4},{16,24},{20,28},{24,16},{28,20},{1,9},{5... | collective-permute-start | bytes 196616 | tf_op jit(solution)/shard_map/ppermute | solution.py:221
  27.2 2.3 %collective-permute-done.10.refs_3_ = f32[128,128]{1,0:T(8,128)S(1)} collective-permute-done((f32[128,128]{1,0:T(8,128)S(1)}, f32[128,128]{1,0:T(8,128)S(1)}, u32[]{:S(2)}, u32[]{:S(2)}) %collective-permute-start.10) | collective-permute-done | bytes 65568 | tf_op jit(solution)/shard_map/ppermute | solution.py:221
  29.5 0.3 collective-permute-done.9.refs_2_
  29.8 0.7 %collective-permute-done.8.refs_1_ = f32[128,128]{1,0:T(8,128)S(1)} collective-permute-done((f32[128,128]{1,0:T(8,128)S(1)}, f32[128,128]{1,0:T(8,128)S(1)}, u32[]{:S(2)}, u32[]{:S(2)}) %collective-permute-start.8) | collective-permute-done | bytes 65568 | tf_op jit(solution)/shard_map/ppermute | solution.py:221
  30.5 4.8 %rotate.1 = f32[32,512]{1,0:T(8,128)} custom-call(f32[128,128]{1,0:T(8,128)S(1)} %sum.1.refs_0_, f32[128,128]{1,0:T(8,128)S(1)} %collective-permute-done.8.refs_1_, f32[128,128]{1,0:T(8,128)S(1)} %collective-permute-done.9.refs_2_, f32[128,128]{1,0:T(8,128)S(1)} %collective-permute-done.10.refs_3_, bf16[2,128,512]{2,1,0:T(8,128)(2,1)S(1)} %get-tuple-element.12.refs_4_), custom_call_target="tpu_custom_call" | custom-call | tf_op jit(solution)/shard_map/rotate/pallas_call | solution.py:324
  (8 shorter events, 0.1 us)
Async XLA Ops:
  0.0 7.2 %copy-start = (f32[32,512]{1,0:T(8,128)S(1)}, f32[32,512]{1,0:T(8,128)}, u32[]{:S(2)}) copy-start(f32[32,512]{1,0:T(8,128)} %refs_5_.3) | copy-start | bytes 196612
  0.0 7.2 %collective-permute-start.2 = (f32[32,512]{1,0:T(8,128)}, f32[32,512]{1,0:T(8,128)S(1)}, u32[]{:S(2)}, u32[]{:S(2)}) collective-permute-start(f32[32,512]{1,0:T(8,128)} %refs_5_.3), channel_id=1, source_target_pairs={{0,4},{4,0},{8,12},{12,8},{16,20},{20,16},{24,28},{28,24},{1,5},{5... | collective-permute-start | bytes 196616 | tf_op jit(solution)/shard_map/ppermute | solution.py:221
  0.5 7.2 %collective-permute-start = (f32[32,512]{1,0:T(8,128)}, f32[32,512]{1,0:T(8,128)S(1)}, u32[]{:S(2)}, u32[]{:S(2)}) collective-permute-start(f32[32,512]{1,0:T(8,128)} %refs_5_.3), channel_id=1, source_target_pairs={{0,28},{4,8},{8,4},{12,16},{16,12},{20,24},{24,20},{28,0},{1,29},{... | collective-permute-start | bytes 196616 | tf_op jit(solution)/shard_map/ppermute | solution.py:240
  7.5 3.0 %collective-permute-start.3 = (f32[32,256]{1,0:T(8,128)S(1)}, f32[32,256]{1,0:T(8,128)S(1)}, u32[]{:S(2)}, u32[]{:S(2)}) collective-permute-start(f32[32,256]{1,0:T(8,128)S(1)} %first_near.1.refs_1_), channel_id=1, source_target_pairs={{0,4},{4,0},{8,12},{12,8},{16,20},{20,16},{24,28},{28,24},{1,5},{5... | collective-permute-start | bytes 98312 | tf_op jit(solution)/shard_map/ppermute | solution.py:221
  7.9 4.4 %collective-permute-start.1 = (f32[32,256]{1,0:T(8,128)S(1)}, f32[32,256]{1,0:T(8,128)S(1)}, u32[]{:S(2)}, u32[]{:S(2)}) collective-permute-start(f32[32,256]{1,0:T(8,128)S(1)} %first_far.1.refs_2_), channel_id=1, source_target_pairs={{0,28},{4,8},{8,4},{12,16},{16,12},{20,24},{24,20},{28,0},{1,29},{... | collective-permute-start | bytes 98312 | tf_op jit(solution)/shard_map/ppermute | solution.py:240
  12.7 6.6 %collective-permute-start.6 = (f32[32,512]{1,0:T(8,128)S(1)}, f32[32,512]{1,0:T(8,128)S(1)}, u32[]{:S(2)}, u32[]{:S(2)}) collective-permute-start(f32[32,512]{1,0:T(8,128)S(1)} %second_far.1.refs_0_), channel_id=1, source_target_pairs={{0,3},{1,2},{2,1},{3,0},{4,7},{5,6},{6,5},{7,4},{8,11},{9,10},{10,... | collective-permute-start | bytes 196616 | tf_op jit(solution)/shard_map/ppermute | solution.py:221
  16.3 4.8 %collective-permute-start.5 = (f32[32,512]{1,0:T(8,128)S(1)}, f32[32,512]{1,0:T(8,128)S(1)}, u32[]{:S(2)}, u32[]{:S(2)}) collective-permute-start(f32[32,512]{1,0:T(8,128)S(1)} %second_far.1.refs_0_), channel_id=1, source_target_pairs={{0,1},{1,0},{2,3},{3,2},{4,5},{5,4},{6,7},{7,6},{8,9},{9,8},{10,11... | collective-permute-start | bytes 196616 | tf_op jit(solution)/shard_map/ppermute | solution.py:221
  16.3 5.6 %collective-permute-start.4 = (f32[32,512]{1,0:T(8,128)S(1)}, f32[32,512]{1,0:T(8,128)S(1)}, u32[]{:S(2)}, u32[]{:S(2)}) collective-permute-start(f32[32,512]{1,0:T(8,128)S(1)} %second_far.1.refs_0_), channel_id=1, source_target_pairs={{0,2},{1,3},{2,0},{3,1},{4,6},{5,7},{6,4},{7,5},{8,10},{9,11},{10,... | collective-permute-start | bytes 196616 | tf_op jit(solution)/shard_map/ppermute | solution.py:221
  22.3 1.3 %collective-permute-start.7 = (f32[128,128]{1,0:T(8,128)S(1)}, f32[128,128]{1,0:T(8,128)S(1)}, u32[]{:S(2)}, u32[]{:S(2)}) collective-permute-start(f32[128,128]{1,0:T(8,128)S(1)} %get-tuple-element.11.refs_0_), channel_id=1, source_target_pairs={{0,4},{4,0},{8,12},{12,8},{16,20},{20,16},{24,28},{28,24},{1,5},{5... | collective-permute-start | bytes 196616 | tf_op jit(solution)/shard_map/ppermute | solution.py:221
  23.6 5.9 %collective-permute-start.10 = (f32[128,128]{1,0:T(8,128)S(1)}, f32[128,128]{1,0:T(8,128)S(1)}, u32[]{:S(2)}, u32[]{:S(2)}) collective-permute-start(f32[128,128]{1,0:T(8,128)S(1)} %sum.1.refs_0_), channel_id=1, source_target_pairs={{0,24},{4,28},{8,16},{12,20},{16,8},{20,12},{24,0},{28,4},{1,25},{... | collective-permute-start | bytes 196616 | tf_op jit(solution)/shard_map/ppermute | solution.py:221
  23.9 5.9 %collective-permute-start.9 = (f32[128,128]{1,0:T(8,128)S(1)}, f32[128,128]{1,0:T(8,128)S(1)}, u32[]{:S(2)}, u32[]{:S(2)}) collective-permute-start(f32[128,128]{1,0:T(8,128)S(1)} %sum.1.refs_0_), channel_id=1, source_target_pairs={{0,16},{4,20},{8,24},{12,28},{16,0},{20,4},{24,8},{28,12},{1,17},{... | collective-permute-start | bytes 196616 | tf_op jit(solution)/shard_map/ppermute | solution.py:221
  26.3 4.3 %collective-permute-start.8 = (f32[128,128]{1,0:T(8,128)S(1)}, f32[128,128]{1,0:T(8,128)S(1)}, u32[]{:S(2)}, u32[]{:S(2)}) collective-permute-start(f32[128,128]{1,0:T(8,128)S(1)} %sum.1.refs_0_), channel_id=1, source_target_pairs={{0,8},{4,12},{8,0},{12,4},{16,24},{20,28},{24,16},{28,20},{1,9},{5... | collective-permute-start | bytes 196616 | tf_op jit(solution)/shard_map/ppermute | solution.py:221

commit v3 on v2

--- a/solution.py
+++ b/solution.py
@@ -9,7 +9,8 @@
 
 REACH = 4
 LANES = 128
-PANEL = 16
+PANEL = 32
+STEP = 16
 VMEM = pl.BlockSpec(memory_space=pltpu.VMEM)
 SMEM = pl.BlockSpec(memory_space=pltpu.SMEM)
 HBM = pl.BlockSpec(memory_space=pltpu.HBM)
@@ -32,54 +33,67 @@
     return jnp.concatenate([tile[:, half:], tile[:, :half]], axis=1)
 
 
-def prepare(there, offsets_there, *refs):
-    near_band, far_band, matrix, near_sums, far_sums, offsets, sems = refs
-    odd = lax.axis_index("nodes") % 2 == 1
-    count, size, depth = matrix.shape
+def prepare(there, offsets_there, near_band, far_band, blocks, offsets, sems, *sums):
+    count = there.shape[0]
+    rows = half_rows(True, count) + half_rows(False, count)
+    copies = [pltpu.make_async_copy(offsets_there, offsets, sems.at[count])]
+    copies += [
+        pltpu.make_async_copy(there.at[b], blocks.at[r], sems.at[r]) for r, b in enumerate(rows)
+    ]
+    for copy in copies:
+        copy.start()
+    for one in sums:
+        one[...] = jnp.zeros(one.shape, jnp.float32)
+    for copy in copies:
+        copy.wait()
+    add_up(blocks, rows, offsets, sums)
+    make_band(sums[:REACH], near_band)
+    make_band(sums[REACH:], far_band)
+
+
+def half_rows(is_near, count):
+    begin = jnp.where(before_own(is_near), 0, count - REACH)
+    return [begin + r for r in range(REACH)]
+
+
+def add_up(blocks, rows, offsets, sums):
+    _, size, depth = blocks.shape
     neighbours = depth // size
-    span = 2 * REACH + 1
-    begin = jnp.where(odd, 0, count - REACH)
-
-    def copy(b):
-        return pltpu.make_async_copy(there.at[b], matrix.at[b], sems.at[b])
-
-    distances = pltpu.make_async_copy(offsets_there, offsets, sems.at[count])
-    distances.start()
-    rows = [lax.rem(begin + r, count) for r in range(count)]
-    for b in rows:
-        copy(b).start()
-    low_lanes = lax.broadcasted_iota(jnp.int32, (size, LANES), 1) < size
-    for sums in (near_sums, far_sums):
-        sums[...] = jnp.zeros(sums.shape, jnp.float32)
-    distances.wait()
-    for sums, band, mine in ((near_sums, near_band, rows[:REACH]), (far_sums, far_band, rows[REACH:])):
-        for b in mine:
-            copy(b).wait()
-        for k in range(0, neighbours, 2):
-            for r, b in enumerate(mine):
-                tile = matrix[b, :, k * size : min(k + 2, neighbours) * size].astype(jnp.float32)
-                if tile.shape[1] < LANES:
-                    tile = jnp.concatenate([tile, jnp.zeros_like(tile)], axis=1)
-                for j in range(k, min(k + 2, neighbours)):
-                    place = offsets[b, j] + REACH
-                    sums[r, j - k, place] = sums[r, j - k, place] + tile
-        for r in range(REACH):
-            for t in range(3 * REACH // 2):
-                low, high = 2 * t - r, 2 * t + 1 - r
-                zero = jnp.zeros((size, LANES), jnp.float32)
-                even_low, odd_low = (
-                    (sums[r, 0, low], sums[r, 1, low]) if 0 <= low < span else (zero, zero)
-                )
-                even_high, odd_high = (
-                    (sums[r, 0, high], sums[r, 1, high]) if 0 <= high < span else (zero, zero)
-                )
-                whole = jnp.where(low_lanes, even_low, odd_high) + swapped(
-                    jnp.where(low_lanes, even_high, odd_low)
-                )
-                top, rest = halves(whole)
-                place = (slice(r * size, (r + 1) * size), slice(t * LANES, (t + 1) * LANES))
-                band[(0, *place)] = top
-                band[(1, *place)] = rest
+    half = size // 2
+    low_lanes = lax.broadcasted_iota(jnp.int32, (half, LANES), 1) < size
+    for k in range(0, neighbours, 2):
+        for r, (b, one) in enumerate(zip(rows, sums, strict=True)):
+            tile = blocks[r, :, k * size : min(k + 2, neighbours) * size]
+            if tile.shape[1] < LANES:
+                tile = jnp.concatenate([tile, jnp.zeros_like(tile)], axis=1)
+            turned = swapped(tile).astype(jnp.float32)
+            tile = tile.astype(jnp.float32)
+            place = offsets[b, k] + REACH
+            one[place] = one[place] + jnp.where(low_lanes, tile[:half], turned[half:])
+            if k + 1 < neighbours:
+                place = offsets[b, k + 1] + REACH
+                one[place] = one[place] + jnp.where(low_lanes, turned[:half], tile[half:])
+
+
+def make_band(sums, band):
+    span, half, _ = sums[0].shape
+    size = 2 * half
+    low_lanes = lax.broadcasted_iota(jnp.int32, (half, LANES), 1) < size
+    zero = jnp.zeros((half, LANES), jnp.float32)
+    for r, one in enumerate(sums):
+        folded = [one[p] for p in range(span)]
+        turned = [swapped(x) for x in folded]
+        for t in range(3 * REACH // 2):
+            low, high = 2 * t - r, 2 * t + 1 - r
+            even, even_turned = (folded[low], turned[low]) if 0 <= low < span else (zero, zero)
+            odd, odd_turned = (folded[high], turned[high]) if 0 <= high < span else (zero, zero)
+            whole = jnp.concatenate(
+                [jnp.where(low_lanes, even, odd_turned), jnp.where(low_lanes, even_turned, odd)], axis=0
+            )
+            top, rest = halves(whole)
+            place = (slice(r * size, (r + 1) * size), slice(t * LANES, (t + 1) * LANES))
+            band[(0, *place)] = top
+            band[(1, *place)] = rest
 
 
 def side(field, before):
@@ -116,9 +130,17 @@
     return both[:rows] + (both[rows:] + rest)
 
 
-def first_kernel(is_near, rim, own, band, out):
+def first_half(is_near, rim, own, band):
     before = before_own(is_near)
-    out[...] = apply_band(window(own[...], side(rim[...], jnp.logical_not(before)), before), band)
+    return apply_band(window(own[...], side(rim[...], jnp.logical_not(before)), before), band)
+
+
+def first_near(rim, own, band, out):
+    out[...] = first_half(True, rim, own, band)
+
+
+def first_far(rim, own, band, out):
+    out[...] = first_half(False, rim, own, band)
 
 
 def second_half(is_near, rim, near, far, band, earlier_rim, earlier, center, width):
@@ -163,35 +185,67 @@
     refs[-1][...] = functools.reduce(jnp.add, [ref[...] for ref in refs[:-1]])
 
 
+def thirds(x):
+    high = x.astype(jnp.bfloat16)
+    rest = x - high.astype(jnp.float32)
+    middle = rest.astype(jnp.bfloat16)
+    return high, middle, (rest - middle.astype(jnp.float32)).astype(jnp.bfloat16)
+
+
+def outer(left, right):
+    a, b, c = thirds(left)
+    d, e, f = thirds(right)
+    return lax.dot_general(
+        jnp.concatenate([a, a, b, a, b, c], axis=0),
+        jnp.concatenate([d, e, d, f, e, d], axis=0),
+        TN,
+        preferred_element_type=jnp.float32,
+    )
+
+
 def inverse_factor(matrix, inverse):
     order = matrix.shape[0]
-    lane = lax.broadcasted_iota(jnp.int32, (PANEL, order), 1)
-    row = lax.broadcasted_iota(jnp.int32, (PANEL, order), 0)
+    lane = lax.broadcasted_iota(jnp.int32, (8, order), 1)
+    sub = lax.broadcasted_iota(jnp.int32, (8, order), 0)
     for start in range(0, order, PANEL):
         stop = start + PANEL
-        panel = matrix[start:stop]
-        inside = (lane >= start) & (lane < stop)
-        columns = [
-            jnp.broadcast_to(panel[:, start + k : start + k + 1], (PANEL, order))
-            for k in range(PANEL)
-        ]
-        rows = jnp.where(inside, jnp.where(lane == row + start, 1.0, 0.0), panel)
-        for j in range(PANEL):
-            scale = lax.rsqrt(columns[j][j : j + 1])
-            factor = columns[j] * scale
-            pivot = rows[j : j + 1] * scale
-            rows = jnp.where(row > j, rows - factor * pivot, jnp.where(row == j, pivot, rows))
-            for k in range(j + 1, PANEL):
-                columns[k] = columns[k] - factor * (columns[k][j : j + 1] * scale)
-        inverse[start:stop] = jnp.where(lane < stop, rows, 0.0)
+        groups = [matrix[i : i + 8] for i in range(start, stop, 8)]
+        done = []
+        for first in range(start, stop, STEP):
+            after = first + STEP
+            inside = (lane >= first) & (lane < after)
+            columns = [
+                [jnp.broadcast_to(g[:, k : k + 1], g.shape) for g in groups]
+                for k in range(first, after)
+            ]
+            for i, g in enumerate(groups):
+                unit = jnp.where(lane == sub + (first + 8 * i), 1.0, 0.0) if 8 * i < STEP else 0.0
+                groups[i] = jnp.where(inside, unit, g)
+            for j in range(STEP):
+                own, s = divmod(j, 8)
+                scale = lax.rsqrt(columns[j][own][s : s + 1])
+                pivot = groups[own][s : s + 1] * scale
+                heads = [column[own][s : s + 1] * scale for column in columns]
+                for i in range(own, len(groups)):
+                    factor = columns[j][i] * scale
+                    less = groups[i] - factor * pivot
+                    if i == own:
+                        less = jnp.where(sub > s, less, jnp.where(sub == s, pivot, groups[i]))
+                    groups[i] = less
+                    if i > own or s < 7:
+                        for k in range(j + 1, STEP):
+                            columns[k][i] = columns[k][i] - factor * heads[k]
+            beyond = (lane >= after) & (lane < stop)
+            done += [jnp.where(beyond, 0.0, g) for g in groups[: STEP // 8]]
+            groups = groups[STEP // 8 :]
+        rows = jnp.concatenate(done, axis=0)
+        right = lax.broadcasted_iota(jnp.int32, rows.shape, 1) >= stop
+        inverse[start:stop] = jnp.where(right, 0.0, rows)
         if stop < order:
-            beyond = jnp.where(lane >= stop, rows, 0.0)
-            update = lax.dot_general(
-                beyond, rows, TN, precision=lax.Precision.HIGHEST, preferred_element_type=jnp.float32
-            )
+            update = outer(jnp.where(right, rows, 0.0), rows)
             rest = matrix[stop:]
-            rest_lane = lax.broadcasted_iota(jnp.int32, rest.shape, 1)
-            kept = jnp.where((rest_lane >= start) & (rest_lane < stop), 0.0, rest)
+            at = lax.broadcasted_iota(jnp.int32, rest.shape, 1)
+            kept = jnp.where((at >= start) & (at < stop), 0.0, rest)
             matrix[stop:] = kept - update[stop:]
 
 
@@ -214,6 +268,10 @@
 
 def near(x):
     return pltpu.with_memory_space_constraint(x, pltpu.VMEM)
+
+
+def there(x):
+    return pltpu.with_memory_space_constraint(x, pltpu.HBM)
 
 
 def exchange(x, axis, step):
@@ -234,7 +292,7 @@
     part = pltpu.VMEM((rows, half), f32)
     square = pltpu.VMEM((states, states), f32)
     band = pltpu.VMEM((2, REACH * size, 3 * REACH * size), bf16)
-    sums = pltpu.VMEM((REACH, 2, 2 * REACH + 1, size, LANES), f32)
+    sums = pltpu.VMEM((2 * REACH + 1, size // 2, LANES), f32)
 
     def over_links(x):
         return near(lax.ppermute(x, "nodes", off_chip))
@@ -260,23 +318,18 @@
         out_specs=(VMEM, VMEM),
         scratch_shapes=[
             pltpu.VMEM(hamiltonian.shape, bf16),
-            sums,
-            sums,
             pltpu.SMEM(offsets.shape, jnp.int32),
             pltpu.SemaphoreType.DMA((count + 1,)),
+            *[sums] * count,
         ],
         compiler_params=ROOM,
         name="prepare",
-    )(*(pltpu.with_memory_space_constraint(x, pltpu.HBM) for x in (hamiltonian, offsets)))
+    )(there(hamiltonian), there(offsets))
     near_band, far_band = near(near_band), near(far_band)
     own = near(states_block)
-    near_part = call(
-        functools.partial(first_kernel, True), part, near_states, own, near_band, name="first_near"
-    )
+    near_part = call(first_near, part, near_states, own, near_band, name="first_near")
     near_rim = exchange(near_part, "nodes", 1)
-    far_part = call(
-        functools.partial(first_kernel, False), part, far_states, own, far_band, name="first_far"
-    )
+    far_part = call(first_far, part, far_states, own, far_band, name="first_far")
     far_rim = over_links(far_part)
     parts_of = (near_part, far_part)
     scalars = (center, halfwidth)

time: 35.5 us -> 32.9 us (0.927)
  Pallas kernels: 9.59 us -> 7.92 us
  waiting for transfers between devices: 10.9 us -> 9.53 us
  starting transfers between devices: 13.4 us -> 13.9 us
    pallas_call x1, Pallas kernels: 4.76 us -> 3.58 us  [on_device(): pl.pallas_call(rotate_kernel, out_shape=jax.ShapeDtypeStruct((rows, local...]
    ppermute x9, waiting for transfers between devices: 9.46 us -> 8.58 us  [exchange(): return near(lax.ppermute(x, axis, [(i, i ^ step) for i in range(count)]))]
    ppermute x2, starting transfers between devices: 4.82 us -> 5.3 us  [over_links(): return near(lax.ppermute(x, 'nodes', off_chip))]
    pallas_call x1, Pallas kernels: 3.15 us -> 2.67 us  [on_device(): pl.pallas_call(prepare, out_shape=(band, band), in_specs=[HBM, HBM], out_...]
    ppermute x2, waiting for transfers between devices: 1.43 us -> 0.95 us  [over_links(): return near(lax.ppermute(x, 'nodes', off_chip))]
  transfers between devices with their start and end apart: 11 -> 11, of which waited for: 8 -> 6; matrix products, arithmetic and copies ran while one was open for 0% -> 0% of each run, Pallas kernels for 12% -> 11%
where the time goes in v3:
time: 32.9 us; the launch traced here: 32.8 us
  starting transfers between devices  13.9 us (42%)
  waiting for transfers between devices  9.53 us (29%)
  Pallas kernels  7.92 us (24%)
  between operations  1.39 us (4%)
    ppermute x9, starting transfers between devices, exchange(): return near(lax.ppermute(x, axis, [(i, i ^ step) for i in range(count)]))  8.6 us
    ppermute x9, waiting for transfers between devices, exchange(): return near(lax.ppermute(x, axis, [(i, i ^ step) for i in range(count)]))  8.58 us
    ppermute x2, starting transfers between devices, over_links(): return near(lax.ppermute(x, 'nodes', off_chip))  5.3 us
    pallas_call x1, Pallas kernels, on_device(): pl.pallas_call(rotate_kernel, out_shape=jax.ShapeDtypeStruct((rows, local...  3.58 us
    pallas_call x1, Pallas kernels, on_device(): pl.pallas_call(prepare, out_shape=(band, band), in_specs=[HBM, HBM], out_...  2.67 us
    pallas_call x4, Pallas kernels, call(): pl.pallas_call(kernel, out_shape=out, in_specs=[SMEM if x.size == 1 else...  1.37 us
    ppermute x2, waiting for transfers between devices, over_links(): return near(lax.ppermute(x, 'nodes', off_chip))  0.95 us
  transfers between devices with their start and end apart: 11, of which 6 were waited for; matrix products, arithmetic and copies ran while one was open for 0% of the time, Pallas kernels for 11%

profile of v3, /device:TPU:0, one launch (start us, length us, event | category | flops | bytes accessed | tf_op | source)
XLA Modules:
  0.0 32.8 jit_solution(450632283637860046)
XLA Ops:
  0.0 0.5 %collective-permute-start.2 = (f32[32,512]{1,0:T(8,128)}, f32[32,512]{1,0:T(8,128)S(1)}, u32[]{:S(2)}, u32[]{:S(2)}) collective-permute-start(f32[32,512]{1,0:T(8,128)} %refs_5_.3), channel_id=1, source_target_pairs={{0,4},{4,0},{8,12},{12,8},{16,20},{20,16},{24,28},{28,24},{1,5},{5... | collective-permute-start | bytes 196616 | tf_op jit(solution)/shard_map/ppermute | solution.py:279
  0.5 3.6 %collective-permute-start = (f32[32,512]{1,0:T(8,128)}, f32[32,512]{1,0:T(8,128)S(1)}, u32[]{:S(2)}, u32[]{:S(2)}) collective-permute-start(f32[32,512]{1,0:T(8,128)} %refs_5_.3), channel_id=1, source_target_pairs={{0,28},{4,8},{8,4},{12,16},{16,12},{20,24},{24,20},{28,0},{1,29},{... | collective-permute-start | bytes 196616 | tf_op jit(solution)/shard_map/ppermute | solution.py:298
  4.0 2.7 %prepare.1 = (bf16[2,256,768]{2,1,0:T(8,128)(2,1)S(1)}, bf16[2,256,768]{2,1,0:T(8,128)(2,1)S(1)}) custom-call(bf16[8,64,1728]{2,1,0:T(8,128)(2,1)} %there.1, s32[8,27]{1,0:T(8,128)} %offsets_there.1), custom_call_target="tpu_custom_call" | custom-call | tf_op jit(solution)/shard_map/prepare/pallas_call | solution.py:314
  6.7 0.3 %first_near.1.refs_1_ = f32[32,256]{1,0:T(8,128)S(1)} custom-call(f32[32,512]{1,0:T(8,128)S(1)} %collective-permute-done.2.rim.refs_4_, f32[32,512]{1,0:T(8,128)S(1)} %copy-done, bf16[2,256,768]{2,1,0:T(8,128)(2,1)S(1)} %get-tuple-element.10.band.refs_3_), custom_call_target="tpu_custom_call" | custom-call | tf_op jit(solution)/shard_map/first_near/pallas_call | solution.py:302
  7.0 0.1 collective-permute-start.3
  7.1 0.3 %first_far.1.refs_2_ = f32[32,256]{1,0:T(8,128)S(1)} custom-call(f32[32,512]{1,0:T(8,128)S(1)} %collective-permute-done.rim.refs_4_, f32[32,512]{1,0:T(8,128)S(1)} %copy-done, bf16[2,256,768]{2,1,0:T(8,128)(2,1)S(1)} %get-tuple-element.9.band.refs_3_), custom_call_target="tpu_custom_call" | custom-call | tf_op jit(solution)/shard_map/first_far/pallas_call | solution.py:302
  7.5 1.7 %collective-permute-start.1 = (f32[32,256]{1,0:T(8,128)S(1)}, f32[32,256]{1,0:T(8,128)S(1)}, u32[]{:S(2)}, u32[]{:S(2)}) collective-permute-start(f32[32,256]{1,0:T(8,128)S(1)} %first_far.1.refs_2_), channel_id=1, source_target_pairs={{0,28},{4,8},{8,4},{12,16},{16,12},{20,24},{24,20},{28,0},{1,29},{... | collective-permute-start | bytes 98312 | tf_op jit(solution)/shard_map/ppermute | solution.py:298
  10.5 0.4 %second_near.1.refs_8_ = f32[32,256]{1,0:T(8,128)S(1)} custom-call(f32[32,256]{1,0:T(8,128)S(1)} %collective-permute-done.3.refs_0_, f32[32,256]{1,0:T(8,128)S(1)} %first_near.1.refs_1_, f32[32,256]{1,0:T(8,128)S(1)} %first_far.1.refs_2_, bf16[2,256,768]{2,1,0:T(8,128)(2,1)S(1)} %get-tuple-element.10.band.refs_3_, ...), custom_call_target="tpu_custom_call" | custom-call | tf_op jit(solution)/shard_map/second_near/pallas_call | solution.py:302
  10.9 1.0 %collective-permute-done.1.refs_0_ = f32[32,256]{1,0:T(8,128)S(1)} collective-permute-done((f32[32,256]{1,0:T(8,128)S(1)}, f32[32,256]{1,0:T(8,128)S(1)}, u32[]{:S(2)}, u32[]{:S(2)}) %collective-permute-start.1) | collective-permute-done | bytes 32800 | tf_op jit(solution)/shard_map/ppermute | solution.py:298
  11.8 0.4 %second_far.1.refs_0_ = f32[32,512]{1,0:T(8,128)S(1)} custom-call(f32[32,256]{1,0:T(8,128)S(1)} %collective-permute-done.1.refs_0_, f32[32,256]{1,0:T(8,128)S(1)} %first_near.1.refs_1_, f32[32,256]{1,0:T(8,128)S(1)} %first_far.1.refs_2_, bf16[2,256,768]{2,1,0:T(8,128)(2,1)S(1)} %get-tuple-element.9.band.refs_3_, ...), custom_call_target="tpu_custom_call" | custom-call | tf_op jit(solution)/shard_map/second_far/pallas_call | solution.py:302
  12.2 3.7 %collective-permute-start.6 = (f32[32,512]{1,0:T(8,128)S(1)}, f32[32,512]{1,0:T(8,128)S(1)}, u32[]{:S(2)}, u32[]{:S(2)}) collective-permute-start(f32[32,512]{1,0:T(8,128)S(1)} %second_far.1.refs_0_), channel_id=1, source_target_pairs={{0,3},{1,2},{2,1},{3,0},{4,7},{5,6},{6,5},{7,4},{8,11},{9,10},{10,... | collective-permute-start | bytes 196616 | tf_op jit(solution)/shard_map/ppermute | solution.py:279
  15.9 0.8 %collective-permute-start.4 = (f32[32,512]{1,0:T(8,128)S(1)}, f32[32,512]{1,0:T(8,128)S(1)}, u32[]{:S(2)}, u32[]{:S(2)}) collective-permute-start(f32[32,512]{1,0:T(8,128)S(1)} %second_far.1.refs_0_), channel_id=1, source_target_pairs={{0,2},{1,3},{2,0},{3,1},{4,6},{5,7},{6,4},{7,5},{8,10},{9,11},{10,... | collective-permute-start | bytes 196616 | tf_op jit(solution)/shard_map/ppermute | solution.py:279
  16.6 2.3 %collective-permute-done.6.refs_3_ = f32[32,512]{1,0:T(8,128)S(1)} collective-permute-done((f32[32,512]{1,0:T(8,128)S(1)}, f32[32,512]{1,0:T(8,128)S(1)}, u32[]{:S(2)}, u32[]{:S(2)}) %collective-permute-start.6) | collective-permute-done | bytes 65568 | tf_op jit(solution)/shard_map/ppermute | solution.py:279
  18.9 1.8 %collective-permute-done.5.refs_2_ = f32[32,512]{1,0:T(8,128)S(1)} collective-permute-done((f32[32,512]{1,0:T(8,128)S(1)}, f32[32,512]{1,0:T(8,128)S(1)}, u32[]{:S(2)}, u32[]{:S(2)}) %collective-permute-start.5) | collective-permute-done | bytes 65568 | tf_op jit(solution)/shard_map/ppermute | solution.py:279
  20.7 0.9 %collective-permute-done.4.refs_1_ = f32[32,512]{1,0:T(8,128)S(1)} collective-permute-done((f32[32,512]{1,0:T(8,128)S(1)}, f32[32,512]{1,0:T(8,128)S(1)}, u32[]{:S(2)}, u32[]{:S(2)}) %collective-permute-start.4) | collective-permute-done | bytes 65568 | tf_op jit(solution)/shard_map/ppermute | solution.py:279
  21.7 0.3 gram.1
  22.0 0.1 collective-permute-start.7
  22.1 1.2 %collective-permute-done.7.refs_1_ = f32[128,128]{1,0:T(8,128)S(1)} collective-permute-done((f32[128,128]{1,0:T(8,128)S(1)}, f32[128,128]{1,0:T(8,128)S(1)}, u32[]{:S(2)}, u32[]{:S(2)}) %collective-permute-start.7) | collective-permute-done | bytes 65568 | tf_op jit(solution)/shard_map/ppermute | solution.py:279
  23.3 0.4 %collective-permute-start.10 = (f32[128,128]{1,0:T(8,128)S(1)}, f32[128,128]{1,0:T(8,128)S(1)}, u32[]{:S(2)}, u32[]{:S(2)}) collective-permute-start(f32[128,128]{1,0:T(8,128)S(1)} %sum.1.refs_0_), channel_id=1, source_target_pairs={{0,24},{4,28},{8,16},{12,20},{16,8},{20,12},{24,0},{28,4},{1,25},{... | collective-permute-start | bytes 196616 | tf_op jit(solution)/shard_map/ppermute | solution.py:279
  23.7 1.2 %collective-permute-start.9 = (f32[128,128]{1,0:T(8,128)S(1)}, f32[128,128]{1,0:T(8,128)S(1)}, u32[]{:S(2)}, u32[]{:S(2)}) collective-permute-start(f32[128,128]{1,0:T(8,128)S(1)} %sum.1.refs_0_), channel_id=1, source_target_pairs={{0,16},{4,20},{8,24},{12,28},{16,0},{20,4},{24,8},{28,12},{1,17},{... | collective-permute-start | bytes 196616 | tf_op jit(solution)/shard_map/ppermute | solution.py:279
  24.9 2.0 %collective-permute-start.8 = (f32[128,128]{1,0:T(8,128)S(1)}, f32[128,128]{1,0:T(8,128)S(1)}, u32[]{:S(2)}, u32[]{:S(2)}) collective-permute-start(f32[128,128]{1,0:T(8,128)S(1)} %sum.1.refs_0_), channel_id=1, source_target_pairs={{0,8},{4,12},{8,0},{12,4},{16,24},{20,28},{24,16},{28,20},{1,9},{5... | collective-permute-start | bytes 196616 | tf_op jit(solution)/shard_map/ppermute | solution.py:279
  26.9 2.3 %collective-permute-done.10.refs_3_ = f32[128,128]{1,0:T(8,128)S(1)} collective-permute-done((f32[128,128]{1,0:T(8,128)S(1)}, f32[128,128]{1,0:T(8,128)S(1)}, u32[]{:S(2)}, u32[]{:S(2)}) %collective-permute-start.10) | collective-permute-done | bytes 65568 | tf_op jit(solution)/shard_map/ppermute | solution.py:279
  29.1 0.0 collective-permute-done.8.refs_1_
  29.2 3.6 %rotate.1 = f32[32,512]{1,0:T(8,128)} custom-call(f32[128,128]{1,0:T(8,128)S(1)} %sum.1.refs_0_, f32[128,128]{1,0:T(8,128)S(1)} %collective-permute-done.8.refs_1_, f32[128,128]{1,0:T(8,128)S(1)} %collective-permute-done.9.refs_2_, f32[128,128]{1,0:T(8,128)S(1)} %collective-permute-done.10.refs_3_, bf16[2,128,512]{2,1,0:T(8,128)(2,1)S(1)} %get-tuple-element.12.refs_4_), custom_call_target="tpu_custom_call" | custom-call | tf_op jit(solution)/shard_map/rotate/pallas_call | solution.py:377
  (8 shorter events, 0.0 us)
Async XLA Ops:
  0.0 6.7 %copy-start = (f32[32,512]{1,0:T(8,128)S(1)}, f32[32,512]{1,0:T(8,128)}, u32[]{:S(2)}) copy-start(f32[32,512]{1,0:T(8,128)} %refs_5_.3) | copy-start | bytes 196612
  0.0 6.7 %collective-permute-start.2 = (f32[32,512]{1,0:T(8,128)}, f32[32,512]{1,0:T(8,128)S(1)}, u32[]{:S(2)}, u32[]{:S(2)}) collective-permute-start(f32[32,512]{1,0:T(8,128)} %refs_5_.3), channel_id=1, source_target_pairs={{0,4},{4,0},{8,12},{12,8},{16,20},{20,16},{24,28},{28,24},{1,5},{5... | collective-permute-start | bytes 196616 | tf_op jit(solution)/shard_map/ppermute | solution.py:279
  0.5 6.7 %collective-permute-start = (f32[32,512]{1,0:T(8,128)}, f32[32,512]{1,0:T(8,128)S(1)}, u32[]{:S(2)}, u32[]{:S(2)}) collective-permute-start(f32[32,512]{1,0:T(8,128)} %refs_5_.3), channel_id=1, source_target_pairs={{0,28},{4,8},{8,4},{12,16},{16,12},{20,24},{24,20},{28,0},{1,29},{... | collective-permute-start | bytes 196616 | tf_op jit(solution)/shard_map/ppermute | solution.py:298
  7.0 3.5 %collective-permute-start.3 = (f32[32,256]{1,0:T(8,128)S(1)}, f32[32,256]{1,0:T(8,128)S(1)}, u32[]{:S(2)}, u32[]{:S(2)}) collective-permute-start(f32[32,256]{1,0:T(8,128)S(1)} %first_near.1.refs_1_), channel_id=1, source_target_pairs={{0,4},{4,0},{8,12},{12,8},{16,20},{20,16},{24,28},{28,24},{1,5},{5... | collective-permute-start | bytes 98312 | tf_op jit(solution)/shard_map/ppermute | solution.py:279
  7.5 4.4 %collective-permute-start.1 = (f32[32,256]{1,0:T(8,128)S(1)}, f32[32,256]{1,0:T(8,128)S(1)}, u32[]{:S(2)}, u32[]{:S(2)}) collective-permute-start(f32[32,256]{1,0:T(8,128)S(1)} %first_far.1.refs_2_), channel_id=1, source_target_pairs={{0,28},{4,8},{8,4},{12,16},{16,12},{20,24},{24,20},{28,0},{1,29},{... | collective-permute-start | bytes 98312 | tf_op jit(solution)/shard_map/ppermute | solution.py:298
  12.2 6.7 %collective-permute-start.6 = (f32[32,512]{1,0:T(8,128)S(1)}, f32[32,512]{1,0:T(8,128)S(1)}, u32[]{:S(2)}, u32[]{:S(2)}) collective-permute-start(f32[32,512]{1,0:T(8,128)S(1)} %second_far.1.refs_0_), channel_id=1, source_target_pairs={{0,3},{1,2},{2,1},{3,0},{4,7},{5,6},{6,5},{7,4},{8,11},{9,10},{10,... | collective-permute-start | bytes 196616 | tf_op jit(solution)/shard_map/ppermute | solution.py:279
  15.9 4.9 %collective-permute-start.5 = (f32[32,512]{1,0:T(8,128)S(1)}, f32[32,512]{1,0:T(8,128)S(1)}, u32[]{:S(2)}, u32[]{:S(2)}) collective-permute-start(f32[32,512]{1,0:T(8,128)S(1)} %second_far.1.refs_0_), channel_id=1, source_target_pairs={{0,1},{1,0},{2,3},{3,2},{4,5},{5,4},{6,7},{7,6},{8,9},{9,8},{10,11... | collective-permute-start | bytes 196616 | tf_op jit(solution)/shard_map/ppermute | solution.py:279
  15.9 5.8 %collective-permute-start.4 = (f32[32,512]{1,0:T(8,128)S(1)}, f32[32,512]{1,0:T(8,128)S(1)}, u32[]{:S(2)}, u32[]{:S(2)}) collective-permute-start(f32[32,512]{1,0:T(8,128)S(1)} %second_far.1.refs_0_), channel_id=1, source_target_pairs={{0,2},{1,3},{2,0},{3,1},{4,6},{5,7},{6,4},{7,5},{8,10},{9,11},{10,... | collective-permute-start | bytes 196616 | tf_op jit(solution)/shard_map/ppermute | solution.py:279
  22.0 1.3 %collective-permute-start.7 = (f32[128,128]{1,0:T(8,128)S(1)}, f32[128,128]{1,0:T(8,128)S(1)}, u32[]{:S(2)}, u32[]{:S(2)}) collective-permute-start(f32[128,128]{1,0:T(8,128)S(1)} %get-tuple-element.11.refs_0_), channel_id=1, source_target_pairs={{0,4},{4,0},{8,12},{12,8},{16,20},{20,16},{24,28},{28,24},{1,5},{5... | collective-permute-start | bytes 196616 | tf_op jit(solution)/shard_map/ppermute | solution.py:279
  23.3 5.8 %collective-permute-start.10 = (f32[128,128]{1,0:T(8,128)S(1)}, f32[128,128]{1,0:T(8,128)S(1)}, u32[]{:S(2)}, u32[]{:S(2)}) collective-permute-start(f32[128,128]{1,0:T(8,128)S(1)} %sum.1.refs_0_), channel_id=1, source_target_pairs={{0,24},{4,28},{8,16},{12,20},{16,8},{20,12},{24,0},{28,4},{1,25},{... | collective-permute-start | bytes 196616 | tf_op jit(solution)/shard_map/ppermute | solution.py:279
  23.7 5.4 %collective-permute-start.9 = (f32[128,128]{1,0:T(8,128)S(1)}, f32[128,128]{1,0:T(8,128)S(1)}, u32[]{:S(2)}, u32[]{:S(2)}) collective-permute-start(f32[128,128]{1,0:T(8,128)S(1)} %sum.1.refs_0_), channel_id=1, source_target_pairs={{0,16},{4,20},{8,24},{12,28},{16,0},{20,4},{24,8},{28,12},{1,17},{... | collective-permute-start | bytes 196616 | tf_op jit(solution)/shard_map/ppermute | solution.py:279
  24.9 4.3 %collective-permute-start.8 = (f32[128,128]{1,0:T(8,128)S(1)}, f32[128,128]{1,0:T(8,128)S(1)}, u32[]{:S(2)}, u32[]{:S(2)}) collective-permute-start(f32[128,128]{1,0:T(8,128)S(1)} %sum.1.refs_0_), channel_id=1, source_target_pairs={{0,8},{4,12},{8,0},{12,4},{16,24},{20,28},{24,16},{28,20},{1,9},{5... | collective-permute-start | bytes 196616 | tf_op jit(solution)/shard_map/ppermute | solution.py:279

commit v4 on v3

--- a/solution.py
+++ b/solution.py
@@ -9,8 +9,7 @@
 
 REACH = 4
 LANES = 128
-PANEL = 32
-STEP = 16
+PANEL = 16
 VMEM = pl.BlockSpec(memory_space=pltpu.VMEM)
 SMEM = pl.BlockSpec(memory_space=pltpu.SMEM)
 HBM = pl.BlockSpec(memory_space=pltpu.HBM)
@@ -207,46 +206,41 @@
     order = matrix.shape[0]
     lane = lax.broadcasted_iota(jnp.int32, (8, order), 1)
     sub = lax.broadcasted_iota(jnp.int32, (8, order), 0)
+    carried = [matrix[i : i + 8] for i in range(0, PANEL, 8)]
     for start in range(0, order, PANEL):
         stop = start + PANEL
-        groups = [matrix[i : i + 8] for i in range(start, stop, 8)]
-        done = []
-        for first in range(start, stop, STEP):
-            after = first + STEP
-            inside = (lane >= first) & (lane < after)
-            columns = [
-                [jnp.broadcast_to(g[:, k : k + 1], g.shape) for g in groups]
-                for k in range(first, after)
-            ]
-            for i, g in enumerate(groups):
-                unit = jnp.where(lane == sub + (first + 8 * i), 1.0, 0.0) if 8 * i < STEP else 0.0
-                groups[i] = jnp.where(inside, unit, g)
-            for j in range(STEP):
-                own, s = divmod(j, 8)
-                scale = lax.rsqrt(columns[j][own][s : s + 1])
-                pivot = groups[own][s : s + 1] * scale
-                heads = [column[own][s : s + 1] * scale for column in columns]
-                for i in range(own, len(groups)):
-                    factor = columns[j][i] * scale
-                    less = groups[i] - factor * pivot
-                    if i == own:
-                        less = jnp.where(sub > s, less, jnp.where(sub == s, pivot, groups[i]))
-                    groups[i] = less
-                    if i > own or s < 7:
-                        for k in range(j + 1, STEP):
-                            columns[k][i] = columns[k][i] - factor * heads[k]
-            beyond = (lane >= after) & (lane < stop)
-            done += [jnp.where(beyond, 0.0, g) for g in groups[: STEP // 8]]
-            groups = groups[STEP // 8 :]
-        rows = jnp.concatenate(done, axis=0)
+        after = min(stop + PANEL, order)
+        groups = carried + [matrix[i : i + 8] for i in range(stop, after, 8)]
+        inside = (lane >= start) & (lane < stop)
+        columns = [
+            [jnp.broadcast_to(g[:, k : k + 1], g.shape) for g in groups] for k in range(start, stop)
+        ]
+        for i, g in enumerate(groups):
+            unit = jnp.where(lane == sub + (start + 8 * i), 1.0, 0.0) if 8 * i < PANEL else 0.0
+            groups[i] = jnp.where(inside, unit, g)
+        for j in range(PANEL):
+            own, s = divmod(j, 8)
+            scale = lax.rsqrt(columns[j][own][s : s + 1])
+            pivot = groups[own][s : s + 1] * scale
+            heads = [column[own][s : s + 1] * scale for column in columns]
+            for i in range(own, len(groups)):
+                factor = columns[j][i] * scale
+                less = groups[i] - factor * pivot
+                if i == own:
+                    less = jnp.where(sub > s, less, jnp.where(sub == s, pivot, groups[i]))
+                groups[i] = less
+                if i > own or s < 7:
+                    for k in range(j + 1, PANEL):
+                        columns[k][i] = columns[k][i] - factor * heads[k]
+        rows, carried = jnp.concatenate(groups[: PANEL // 8], axis=0), groups[PANEL // 8 :]
         right = lax.broadcasted_iota(jnp.int32, rows.shape, 1) >= stop
         inverse[start:stop] = jnp.where(right, 0.0, rows)
-        if stop < order:
+        if after < order:
             update = outer(jnp.where(right, rows, 0.0), rows)
-            rest = matrix[stop:]
+            rest = matrix[after:]
             at = lax.broadcasted_iota(jnp.int32, rest.shape, 1)
             kept = jnp.where((at >= start) & (at < stop), 0.0, rest)
-            matrix[stop:] = kept - update[stop:]
+            matrix[after:] = kept - update[after:]
 
 
 def rotate_kernel(*refs):

time: 32.9 us -> 32.6 us (level)
  Pallas kernels: 7.92 us -> 7.58 us
    pallas_call x1, Pallas kernels: 3.58 us -> 3.24 us  [on_device(): pl.pallas_call(rotate_kernel, out_shape=jax.ShapeDtypeStruct((rows, local...]
where the time goes in v4:
time: 32.6 us; the launch traced here: 32.4 us
  starting transfers between devices  13.9 us (43%)
  waiting for transfers between devices  9.53 us (29%)
  Pallas kernels  7.58 us (23%)
  between operations  1.39 us (4%)
    ppermute x9, starting transfers between devices, exchange(): return near(lax.ppermute(x, axis, [(i, i ^ step) for i in range(count)]))  8.6 us
    ppermute x9, waiting for transfers between devices, exchange(): return near(lax.ppermute(x, axis, [(i, i ^ step) for i in range(count)]))  8.59 us
    ppermute x2, starting transfers between devices, over_links(): return near(lax.ppermute(x, 'nodes', off_chip))  5.31 us
    pallas_call x1, Pallas kernels, on_device(): pl.pallas_call(rotate_kernel, out_shape=jax.ShapeDtypeStruct((rows, local...  3.24 us
    pallas_call x1, Pallas kernels, on_device(): pl.pallas_call(prepare, out_shape=(band, band), in_specs=[HBM, HBM], out_...  2.66 us
    pallas_call x4, Pallas kernels, call(): pl.pallas_call(kernel, out_shape=out, in_specs=[SMEM if x.size == 1 else...  1.37 us
    ppermute x2, waiting for transfers between devices, over_links(): return near(lax.ppermute(x, 'nodes', off_chip))  0.95 us
  transfers between devices with their start and end apart: 11, of which 6 were waited for; matrix products, arithmetic and copies ran while one was open for 0% of the time, Pallas kernels for 11%

profile of v4, /device:TPU:0, one launch (start us, length us, event | category | flops | bytes accessed | tf_op | source)
XLA Modules:
  0.0 32.4 jit_solution(17757453803843583314)
XLA Ops:
  0.0 0.5 %collective-permute-start.2 = (f32[32,512]{1,0:T(8,128)}, f32[32,512]{1,0:T(8,128)S(1)}, u32[]{:S(2)}, u32[]{:S(2)}) collective-permute-start(f32[32,512]{1,0:T(8,128)} %refs_5_.3), channel_id=1, source_target_pairs={{0,4},{4,0},{8,12},{12,8},{16,20},{20,16},{24,28},{28,24},{1,5},{5... | collective-permute-start | bytes 196616 | tf_op jit(solution)/shard_map/ppermute | solution.py:273
  0.5 3.6 %collective-permute-start = (f32[32,512]{1,0:T(8,128)}, f32[32,512]{1,0:T(8,128)S(1)}, u32[]{:S(2)}, u32[]{:S(2)}) collective-permute-start(f32[32,512]{1,0:T(8,128)} %refs_5_.3), channel_id=1, source_target_pairs={{0,28},{4,8},{8,4},{12,16},{16,12},{20,24},{24,20},{28,0},{1,29},{... | collective-permute-start | bytes 196616 | tf_op jit(solution)/shard_map/ppermute | solution.py:292
  4.0 2.7 %prepare.1 = (bf16[2,256,768]{2,1,0:T(8,128)(2,1)S(1)}, bf16[2,256,768]{2,1,0:T(8,128)(2,1)S(1)}) custom-call(bf16[8,64,1728]{2,1,0:T(8,128)(2,1)} %there.1, s32[8,27]{1,0:T(8,128)} %offsets_there.1), custom_call_target="tpu_custom_call" | custom-call | tf_op jit(solution)/shard_map/prepare/pallas_call | solution.py:308
  6.7 0.3 %first_near.1.refs_1_ = f32[32,256]{1,0:T(8,128)S(1)} custom-call(f32[32,512]{1,0:T(8,128)S(1)} %collective-permute-done.2.rim.refs_4_, f32[32,512]{1,0:T(8,128)S(1)} %copy-done, bf16[2,256,768]{2,1,0:T(8,128)(2,1)S(1)} %get-tuple-element.10.band.refs_3_), custom_call_target="tpu_custom_call" | custom-call | tf_op jit(solution)/shard_map/first_near/pallas_call | solution.py:296
  7.0 0.1 collective-permute-start.3
  7.1 0.3 %first_far.1.refs_2_ = f32[32,256]{1,0:T(8,128)S(1)} custom-call(f32[32,512]{1,0:T(8,128)S(1)} %collective-permute-done.rim.refs_4_, f32[32,512]{1,0:T(8,128)S(1)} %copy-done, bf16[2,256,768]{2,1,0:T(8,128)(2,1)S(1)} %get-tuple-element.9.band.refs_3_), custom_call_target="tpu_custom_call" | custom-call | tf_op jit(solution)/shard_map/first_far/pallas_call | solution.py:296
  7.4 1.8 %collective-permute-start.1 = (f32[32,256]{1,0:T(8,128)S(1)}, f32[32,256]{1,0:T(8,128)S(1)}, u32[]{:S(2)}, u32[]{:S(2)}) collective-permute-start(f32[32,256]{1,0:T(8,128)S(1)} %first_far.1.refs_2_), channel_id=1, source_target_pairs={{0,28},{4,8},{8,4},{12,16},{16,12},{20,24},{24,20},{28,0},{1,29},{... | collective-permute-start | bytes 98312 | tf_op jit(solution)/shard_map/ppermute | solution.py:292
  10.5 0.4 %second_near.1.refs_8_ = f32[32,256]{1,0:T(8,128)S(1)} custom-call(f32[32,256]{1,0:T(8,128)S(1)} %collective-permute-done.3.refs_0_, f32[32,256]{1,0:T(8,128)S(1)} %first_near.1.refs_1_, f32[32,256]{1,0:T(8,128)S(1)} %first_far.1.refs_2_, bf16[2,256,768]{2,1,0:T(8,128)(2,1)S(1)} %get-tuple-element.10.band.refs_3_, ...), custom_call_target="tpu_custom_call" | custom-call | tf_op jit(solution)/shard_map/second_near/pallas_call | solution.py:296
  10.9 0.9 %collective-permute-done.1.refs_0_ = f32[32,256]{1,0:T(8,128)S(1)} collective-permute-done((f32[32,256]{1,0:T(8,128)S(1)}, f32[32,256]{1,0:T(8,128)S(1)}, u32[]{:S(2)}, u32[]{:S(2)}) %collective-permute-start.1) | collective-permute-done | bytes 32800 | tf_op jit(solution)/shard_map/ppermute | solution.py:292
  11.8 0.4 %second_far.1.refs_0_ = f32[32,512]{1,0:T(8,128)S(1)} custom-call(f32[32,256]{1,0:T(8,128)S(1)} %collective-permute-done.1.refs_0_, f32[32,256]{1,0:T(8,128)S(1)} %first_near.1.refs_1_, f32[32,256]{1,0:T(8,128)S(1)} %first_far.1.refs_2_, bf16[2,256,768]{2,1,0:T(8,128)(2,1)S(1)} %get-tuple-element.9.band.refs_3_, ...), custom_call_target="tpu_custom_call" | custom-call | tf_op jit(solution)/shard_map/second_far/pallas_call | solution.py:296
  12.2 3.7 %collective-permute-start.6 = (f32[32,512]{1,0:T(8,128)S(1)}, f32[32,512]{1,0:T(8,128)S(1)}, u32[]{:S(2)}, u32[]{:S(2)}) collective-permute-start(f32[32,512]{1,0:T(8,128)S(1)} %second_far.1.refs_0_), channel_id=1, source_target_pairs={{0,3},{1,2},{2,1},{3,0},{4,7},{5,6},{6,5},{7,4},{8,11},{9,10},{10,... | collective-permute-start | bytes 196616 | tf_op jit(solution)/shard_map/ppermute | solution.py:273
  15.9 0.8 %collective-permute-start.4 = (f32[32,512]{1,0:T(8,128)S(1)}, f32[32,512]{1,0:T(8,128)S(1)}, u32[]{:S(2)}, u32[]{:S(2)}) collective-permute-start(f32[32,512]{1,0:T(8,128)S(1)} %second_far.1.refs_0_), channel_id=1, source_target_pairs={{0,2},{1,3},{2,0},{3,1},{4,6},{5,7},{6,4},{7,5},{8,10},{9,11},{10,... | collective-permute-start | bytes 196616 | tf_op jit(solution)/shard_map/ppermute | solution.py:273
  16.6 2.3 %collective-permute-done.6.refs_3_ = f32[32,512]{1,0:T(8,128)S(1)} collective-permute-done((f32[32,512]{1,0:T(8,128)S(1)}, f32[32,512]{1,0:T(8,128)S(1)}, u32[]{:S(2)}, u32[]{:S(2)}) %collective-permute-start.6) | collective-permute-done | bytes 65568 | tf_op jit(solution)/shard_map/ppermute | solution.py:273
  18.9 1.8 %collective-permute-done.5.refs_2_ = f32[32,512]{1,0:T(8,128)S(1)} collective-permute-done((f32[32,512]{1,0:T(8,128)S(1)}, f32[32,512]{1,0:T(8,128)S(1)}, u32[]{:S(2)}, u32[]{:S(2)}) %collective-permute-start.5) | collective-permute-done | bytes 65568 | tf_op jit(solution)/shard_map/ppermute | solution.py:273
  20.7 0.9 %collective-permute-done.4.refs_1_ = f32[32,512]{1,0:T(8,128)S(1)} collective-permute-done((f32[32,512]{1,0:T(8,128)S(1)}, f32[32,512]{1,0:T(8,128)S(1)}, u32[]{:S(2)}, u32[]{:S(2)}) %collective-permute-start.4) | collective-permute-done | bytes 65568 | tf_op jit(solution)/shard_map/ppermute | solution.py:273
  21.7 0.3 gram.1
  22.0 0.1 collective-permute-start.7
  22.1 1.2 %collective-permute-done.7.refs_1_ = f32[128,128]{1,0:T(8,128)S(1)} collective-permute-done((f32[128,128]{1,0:T(8,128)S(1)}, f32[128,128]{1,0:T(8,128)S(1)}, u32[]{:S(2)}, u32[]{:S(2)}) %collective-permute-start.7) | collective-permute-done | bytes 65568 | tf_op jit(solution)/shard_map/ppermute | solution.py:273
  23.3 0.4 %collective-permute-start.10 = (f32[128,128]{1,0:T(8,128)S(1)}, f32[128,128]{1,0:T(8,128)S(1)}, u32[]{:S(2)}, u32[]{:S(2)}) collective-permute-start(f32[128,128]{1,0:T(8,128)S(1)} %sum.1.refs_0_), channel_id=1, source_target_pairs={{0,24},{4,28},{8,16},{12,20},{16,8},{20,12},{24,0},{28,4},{1,25},{... | collective-permute-start | bytes 196616 | tf_op jit(solution)/shard_map/ppermute | solution.py:273
  23.7 1.2 %collective-permute-start.9 = (f32[128,128]{1,0:T(8,128)S(1)}, f32[128,128]{1,0:T(8,128)S(1)}, u32[]{:S(2)}, u32[]{:S(2)}) collective-permute-start(f32[128,128]{1,0:T(8,128)S(1)} %sum.1.refs_0_), channel_id=1, source_target_pairs={{0,16},{4,20},{8,24},{12,28},{16,0},{20,4},{24,8},{28,12},{1,17},{... | collective-permute-start | bytes 196616 | tf_op jit(solution)/shard_map/ppermute | solution.py:273
  24.9 2.0 %collective-permute-start.8 = (f32[128,128]{1,0:T(8,128)S(1)}, f32[128,128]{1,0:T(8,128)S(1)}, u32[]{:S(2)}, u32[]{:S(2)}) collective-permute-start(f32[128,128]{1,0:T(8,128)S(1)} %sum.1.refs_0_), channel_id=1, source_target_pairs={{0,8},{4,12},{8,0},{12,4},{16,24},{20,28},{24,16},{28,20},{1,9},{5... | collective-permute-start | bytes 196616 | tf_op jit(solution)/shard_map/ppermute | solution.py:273
  26.9 2.3 %collective-permute-done.10.refs_3_ = f32[128,128]{1,0:T(8,128)S(1)} collective-permute-done((f32[128,128]{1,0:T(8,128)S(1)}, f32[128,128]{1,0:T(8,128)S(1)}, u32[]{:S(2)}, u32[]{:S(2)}) %collective-permute-start.10) | collective-permute-done | bytes 65568 | tf_op jit(solution)/shard_map/ppermute | solution.py:273
  29.1 0.0 collective-permute-done.8.refs_1_
  29.2 3.2 %rotate.1 = f32[32,512]{1,0:T(8,128)} custom-call(f32[128,128]{1,0:T(8,128)S(1)} %sum.1.refs_0_, f32[128,128]{1,0:T(8,128)S(1)} %collective-permute-done.8.refs_1_, f32[128,128]{1,0:T(8,128)S(1)} %collective-permute-done.9.refs_2_, f32[128,128]{1,0:T(8,128)S(1)} %collective-permute-done.10.refs_3_, bf16[2,128,512]{2,1,0:T(8,128)(2,1)S(1)} %get-tuple-element.12.refs_4_), custom_call_target="tpu_custom_call" | custom-call | tf_op jit(solution)/shard_map/rotate/pallas_call | solution.py:371
  (8 shorter events, 0.0 us)
Async XLA Ops:
  0.0 6.7 %copy-start = (f32[32,512]{1,0:T(8,128)S(1)}, f32[32,512]{1,0:T(8,128)}, u32[]{:S(2)}) copy-start(f32[32,512]{1,0:T(8,128)} %refs_5_.3) | copy-start | bytes 196612
  0.0 6.7 %collective-permute-start.2 = (f32[32,512]{1,0:T(8,128)}, f32[32,512]{1,0:T(8,128)S(1)}, u32[]{:S(2)}, u32[]{:S(2)}) collective-permute-start(f32[32,512]{1,0:T(8,128)} %refs_5_.3), channel_id=1, source_target_pairs={{0,4},{4,0},{8,12},{12,8},{16,20},{20,16},{24,28},{28,24},{1,5},{5... | collective-permute-start | bytes 196616 | tf_op jit(solution)/shard_map/ppermute | solution.py:273
  0.5 6.7 %collective-permute-start = (f32[32,512]{1,0:T(8,128)}, f32[32,512]{1,0:T(8,128)S(1)}, u32[]{:S(2)}, u32[]{:S(2)}) collective-permute-start(f32[32,512]{1,0:T(8,128)} %refs_5_.3), channel_id=1, source_target_pairs={{0,28},{4,8},{8,4},{12,16},{16,12},{20,24},{24,20},{28,0},{1,29},{... | collective-permute-start | bytes 196616 | tf_op jit(solution)/shard_map/ppermute | solution.py:292
  7.0 3.5 %collective-permute-start.3 = (f32[32,256]{1,0:T(8,128)S(1)}, f32[32,256]{1,0:T(8,128)S(1)}, u32[]{:S(2)}, u32[]{:S(2)}) collective-permute-start(f32[32,256]{1,0:T(8,128)S(1)} %first_near.1.refs_1_), channel_id=1, source_target_pairs={{0,4},{4,0},{8,12},{12,8},{16,20},{20,16},{24,28},{28,24},{1,5},{5... | collective-permute-start | bytes 98312 | tf_op jit(solution)/shard_map/ppermute | solution.py:273
  7.4 4.4 %collective-permute-start.1 = (f32[32,256]{1,0:T(8,128)S(1)}, f32[32,256]{1,0:T(8,128)S(1)}, u32[]{:S(2)}, u32[]{:S(2)}) collective-permute-start(f32[32,256]{1,0:T(8,128)S(1)} %first_far.1.refs_2_), channel_id=1, source_target_pairs={{0,28},{4,8},{8,4},{12,16},{16,12},{20,24},{24,20},{28,0},{1,29},{... | collective-permute-start | bytes 98312 | tf_op jit(solution)/shard_map/ppermute | solution.py:292
  12.2 6.8 %collective-permute-start.6 = (f32[32,512]{1,0:T(8,128)S(1)}, f32[32,512]{1,0:T(8,128)S(1)}, u32[]{:S(2)}, u32[]{:S(2)}) collective-permute-start(f32[32,512]{1,0:T(8,128)S(1)} %second_far.1.refs_0_), channel_id=1, source_target_pairs={{0,3},{1,2},{2,1},{3,0},{4,7},{5,6},{6,5},{7,4},{8,11},{9,10},{10,... | collective-permute-start | bytes 196616 | tf_op jit(solution)/shard_map/ppermute | solution.py:273
  15.8 4.9 %collective-permute-start.5 = (f32[32,512]{1,0:T(8,128)S(1)}, f32[32,512]{1,0:T(8,128)S(1)}, u32[]{:S(2)}, u32[]{:S(2)}) collective-permute-start(f32[32,512]{1,0:T(8,128)S(1)} %second_far.1.refs_0_), channel_id=1, source_target_pairs={{0,1},{1,0},{2,3},{3,2},{4,5},{5,4},{6,7},{7,6},{8,9},{9,8},{10,11... | collective-permute-start | bytes 196616 | tf_op jit(solution)/shard_map/ppermute | solution.py:273
  15.9 5.8 %collective-permute-start.4 = (f32[32,512]{1,0:T(8,128)S(1)}, f32[32,512]{1,0:T(8,128)S(1)}, u32[]{:S(2)}, u32[]{:S(2)}) collective-permute-start(f32[32,512]{1,0:T(8,128)S(1)} %second_far.1.refs_0_), channel_id=1, source_target_pairs={{0,2},{1,3},{2,0},{3,1},{4,6},{5,7},{6,4},{7,5},{8,10},{9,11},{10,... | collective-permute-start | bytes 196616 | tf_op jit(solution)/shard_map/ppermute | solution.py:273
  22.0 1.3 %collective-permute-start.7 = (f32[128,128]{1,0:T(8,128)S(1)}, f32[128,128]{1,0:T(8,128)S(1)}, u32[]{:S(2)}, u32[]{:S(2)}) collective-permute-start(f32[128,128]{1,0:T(8,128)S(1)} %get-tuple-element.11.refs_0_), channel_id=1, source_target_pairs={{0,4},{4,0},{8,12},{12,8},{16,20},{20,16},{24,28},{28,24},{1,5},{5... | collective-permute-start | bytes 196616 | tf_op jit(solution)/shard_map/ppermute | solution.py:273
  23.3 5.8 %collective-permute-start.10 = (f32[128,128]{1,0:T(8,128)S(1)}, f32[128,128]{1,0:T(8,128)S(1)}, u32[]{:S(2)}, u32[]{:S(2)}) collective-permute-start(f32[128,128]{1,0:T(8,128)S(1)} %sum.1.refs_0_), channel_id=1, source_target_pairs={{0,24},{4,28},{8,16},{12,20},{16,8},{20,12},{24,0},{28,4},{1,25},{... | collective-permute-start | bytes 196616 | tf_op jit(solution)/shard_map/ppermute | solution.py:273
  23.7 5.4 %collective-permute-start.9 = (f32[128,128]{1,0:T(8,128)S(1)}, f32[128,128]{1,0:T(8,128)S(1)}, u32[]{:S(2)}, u32[]{:S(2)}) collective-permute-start(f32[128,128]{1,0:T(8,128)S(1)} %sum.1.refs_0_), channel_id=1, source_target_pairs={{0,16},{4,20},{8,24},{12,28},{16,0},{20,4},{24,8},{28,12},{1,17},{... | collective-permute-start | bytes 196616 | tf_op jit(solution)/shard_map/ppermute | solution.py:273
  24.9 4.3 %collective-permute-start.8 = (f32[128,128]{1,0:T(8,128)S(1)}, f32[128,128]{1,0:T(8,128)S(1)}, u32[]{:S(2)}, u32[]{:S(2)}) collective-permute-start(f32[128,128]{1,0:T(8,128)S(1)} %sum.1.refs_0_), channel_id=1, source_target_pairs={{0,8},{4,12},{8,0},{12,4},{16,24},{20,28},{24,16},{28,20},{1,9},{5... | collective-permute-start | bytes 196616 | tf_op jit(solution)/shard_map/ppermute | solution.py:273

commit v5 on v4

--- a/solution.py
+++ b/solution.py
@@ -160,18 +160,17 @@
 
 def second_far(*refs):
     *rest, done, out = refs
-    out[...] = joined(done[...], second_half(False, *rest), before_own(True))
+    out[...] = stacked(joined(done[...], second_half(False, *rest), before_own(True)))
 
 
 def gram_kernel(total_nodes, steps, *refs):
     parts, (gathered, gram) = refs[:-2], refs[-2:]
-    rows = parts[0].shape[0]
+    rows = parts[0].shape[0] // 2
     me = lax.axis_index("states")
     for step, part in zip(steps, parts, strict=True):
         place = pl.ds(pl.multiple_of((me ^ step) * rows, rows), rows)
-        high, low = halves(part[...])
-        gathered[0, place] = high
-        gathered[1, place] = low
+        gathered[0, place] = part[:rows]
+        gathered[1, place] = part[rows:]
     states = len(parts) * rows
     both = gathered[...].reshape(2 * states, -1)
     terms = lax.dot_general(both, both, NT, preferred_element_type=jnp.float32)
@@ -332,7 +331,7 @@
     )
     second = call(
         second_far,
-        field,
+        pltpu.VMEM((2 * rows, local), bf16),
         far_rim,
         *parts_of,
         far_band,

time: 32.6 us -> 32.6 us (level)
  no operation moved by 1% of the time
where the time goes in v5:
time: 32.6 us; the launch traced here: 32.4 us
  starting transfers between devices  13.9 us (43%)
  waiting for transfers between devices  9.53 us (29%)
  Pallas kernels  7.57 us (23%)
  between operations  1.39 us (4%)
    ppermute x9, starting transfers between devices, exchange(): return near(lax.ppermute(x, axis, [(i, i ^ step) for i in range(count)]))  8.6 us
    ppermute x9, waiting for transfers between devices, exchange(): return near(lax.ppermute(x, axis, [(i, i ^ step) for i in range(count)]))  8.58 us
    ppermute x2, starting transfers between devices, over_links(): return near(lax.ppermute(x, 'nodes', off_chip))  5.31 us
    pallas_call x1, Pallas kernels, on_device(): pl.pallas_call(rotate_kernel, out_shape=jax.ShapeDtypeStruct((rows, local...  3.24 us
    pallas_call x1, Pallas kernels, on_device(): pl.pallas_call(prepare, out_shape=(band, band), in_specs=[HBM, HBM], out_...  2.66 us
    pallas_call x4, Pallas kernels, call(): pl.pallas_call(kernel, out_shape=out, in_specs=[SMEM if x.size == 1 else...  1.38 us
    ppermute x2, waiting for transfers between devices, over_links(): return near(lax.ppermute(x, 'nodes', off_chip))  0.95 us
  transfers between devices with their start and end apart: 11, of which 6 were waited for; matrix products, arithmetic and copies ran while one was open for 0% of the time, Pallas kernels for 11%

profile of v5, /device:TPU:0, one launch (start us, length us, event | category | flops | bytes accessed | tf_op | source)
XLA Modules:
  0.0 32.4 jit_solution(18046473905341923747)
XLA Ops:
  0.0 0.5 %collective-permute-start.2 = (f32[32,512]{1,0:T(8,128)}, f32[32,512]{1,0:T(8,128)S(1)}, u32[]{:S(2)}, u32[]{:S(2)}) collective-permute-start(f32[32,512]{1,0:T(8,128)} %refs_5_.3), channel_id=1, source_target_pairs={{0,4},{4,0},{8,12},{12,8},{16,20},{20,16},{24,28},{28,24},{1,5},{5... | collective-permute-start | bytes 196616 | tf_op jit(solution)/shard_map/ppermute | solution.py:272
  0.5 3.6 %collective-permute-start = (f32[32,512]{1,0:T(8,128)}, f32[32,512]{1,0:T(8,128)S(1)}, u32[]{:S(2)}, u32[]{:S(2)}) collective-permute-start(f32[32,512]{1,0:T(8,128)} %refs_5_.3), channel_id=1, source_target_pairs={{0,28},{4,8},{8,4},{12,16},{16,12},{20,24},{24,20},{28,0},{1,29},{... | collective-permute-start | bytes 196616 | tf_op jit(solution)/shard_map/ppermute | solution.py:291
  4.0 2.7 %prepare.1 = (bf16[2,256,768]{2,1,0:T(8,128)(2,1)S(1)}, bf16[2,256,768]{2,1,0:T(8,128)(2,1)S(1)}) custom-call(bf16[8,64,1728]{2,1,0:T(8,128)(2,1)} %there.1, s32[8,27]{1,0:T(8,128)} %offsets_there.1), custom_call_target="tpu_custom_call" | custom-call | tf_op jit(solution)/shard_map/prepare/pallas_call | solution.py:307
  6.7 0.3 %first_near.1.refs_1_ = f32[32,256]{1,0:T(8,128)S(1)} custom-call(f32[32,512]{1,0:T(8,128)S(1)} %collective-permute-done.2.rim.refs_4_, f32[32,512]{1,0:T(8,128)S(1)} %copy-done, bf16[2,256,768]{2,1,0:T(8,128)(2,1)S(1)} %get-tuple-element.10.band.refs_3_), custom_call_target="tpu_custom_call" | custom-call | tf_op jit(solution)/shard_map/first_near/pallas_call | solution.py:295
  7.0 0.1 collective-permute-start.3
  7.1 0.3 %first_far.1.refs_2_ = f32[32,256]{1,0:T(8,128)S(1)} custom-call(f32[32,512]{1,0:T(8,128)S(1)} %collective-permute-done.rim.refs_4_, f32[32,512]{1,0:T(8,128)S(1)} %copy-done, bf16[2,256,768]{2,1,0:T(8,128)(2,1)S(1)} %get-tuple-element.9.band.refs_3_), custom_call_target="tpu_custom_call" | custom-call | tf_op jit(solution)/shard_map/first_far/pallas_call | solution.py:295
  7.5 1.8 %collective-permute-start.1 = (f32[32,256]{1,0:T(8,128)S(1)}, f32[32,256]{1,0:T(8,128)S(1)}, u32[]{:S(2)}, u32[]{:S(2)}) collective-permute-start(f32[32,256]{1,0:T(8,128)S(1)} %first_far.1.refs_2_), channel_id=1, source_target_pairs={{0,28},{4,8},{8,4},{12,16},{16,12},{20,24},{24,20},{28,0},{1,29},{... | collective-permute-start | bytes 98312 | tf_op jit(solution)/shard_map/ppermute | solution.py:291
  10.5 0.4 %second_near.1.refs_8_ = f32[32,256]{1,0:T(8,128)S(1)} custom-call(f32[32,256]{1,0:T(8,128)S(1)} %collective-permute-done.3.refs_0_, f32[32,256]{1,0:T(8,128)S(1)} %first_near.1.refs_1_, f32[32,256]{1,0:T(8,128)S(1)} %first_far.1.refs_2_, bf16[2,256,768]{2,1,0:T(8,128)(2,1)S(1)} %get-tuple-element.10.band.refs_3_, ...), custom_call_target="tpu_custom_call" | custom-call | tf_op jit(solution)/shard_map/second_near/pallas_call | solution.py:295
  10.9 1.0 %collective-permute-done.1.refs_0_ = f32[32,256]{1,0:T(8,128)S(1)} collective-permute-done((f32[32,256]{1,0:T(8,128)S(1)}, f32[32,256]{1,0:T(8,128)S(1)}, u32[]{:S(2)}, u32[]{:S(2)}) %collective-permute-start.1) | collective-permute-done | bytes 32800 | tf_op jit(solution)/shard_map/ppermute | solution.py:291
  11.8 0.4 %second_far.1.refs_0_ = bf16[64,512]{1,0:T(8,128)(2,1)S(1)} custom-call(f32[32,256]{1,0:T(8,128)S(1)} %collective-permute-done.1.refs_0_, f32[32,256]{1,0:T(8,128)S(1)} %first_near.1.refs_1_, f32[32,256]{1,0:T(8,128)S(1)} %first_far.1.refs_2_, bf16[2,256,768]{2,1,0:T(8,128)(2,1)S(1)} %get-tuple-element.9.band.refs_3_, ...), custom_call_target="tpu_custom_call" | custom-call | tf_op jit(solution)/shard_map/second_far/pallas_call | solution.py:295
  12.2 3.7 %collective-permute-start.6 = (bf16[64,512]{1,0:T(8,128)(2,1)S(1)}, bf16[64,512]{1,0:T(8,128)(2,1)S(1)}, u32[]{:S(2)}, u32[]{:S(2)}) collective-permute-start(bf16[64,512]{1,0:T(8,128)(2,1)S(1)} %second_far.1.refs_0_), channel_id=1, source_target_pairs={{0,3},{1,2},{2,1},{3,0},{4,7},{5,6},{6,5},{7,4},{8,11},{9,10},{10,... | collective-permute-start | bytes 196616 | tf_op jit(solution)/shard_map/ppermute | solution.py:272
  15.9 0.8 %collective-permute-start.4 = (bf16[64,512]{1,0:T(8,128)(2,1)S(1)}, bf16[64,512]{1,0:T(8,128)(2,1)S(1)}, u32[]{:S(2)}, u32[]{:S(2)}) collective-permute-start(bf16[64,512]{1,0:T(8,128)(2,1)S(1)} %second_far.1.refs_0_), channel_id=1, source_target_pairs={{0,2},{1,3},{2,0},{3,1},{4,6},{5,7},{6,4},{7,5},{8,10},{9,11},{10,... | collective-permute-start | bytes 196616 | tf_op jit(solution)/shard_map/ppermute | solution.py:272
  16.7 2.3 %collective-permute-done.6.refs_3_ = bf16[64,512]{1,0:T(8,128)(2,1)S(1)} collective-permute-done((bf16[64,512]{1,0:T(8,128)(2,1)S(1)}, bf16[64,512]{1,0:T(8,128)(2,1)S(1)}, u32[]{:S(2)}, u32[]{:S(2)}) %collective-permute-start.6) | collective-permute-done | bytes 65568 | tf_op jit(solution)/shard_map/ppermute | solution.py:272
  18.9 1.8 %collective-permute-done.5.refs_2_ = bf16[64,512]{1,0:T(8,128)(2,1)S(1)} collective-permute-done((bf16[64,512]{1,0:T(8,128)(2,1)S(1)}, bf16[64,512]{1,0:T(8,128)(2,1)S(1)}, u32[]{:S(2)}, u32[]{:S(2)}) %collective-permute-start.5) | collective-permute-done | bytes 65568 | tf_op jit(solution)/shard_map/ppermute | solution.py:272
  20.8 0.9 %collective-permute-done.4.refs_1_ = bf16[64,512]{1,0:T(8,128)(2,1)S(1)} collective-permute-done((bf16[64,512]{1,0:T(8,128)(2,1)S(1)}, bf16[64,512]{1,0:T(8,128)(2,1)S(1)}, u32[]{:S(2)}, u32[]{:S(2)}) %collective-permute-start.4) | collective-permute-done | bytes 65568 | tf_op jit(solution)/shard_map/ppermute | solution.py:272
  21.7 0.3 gram.1
  22.0 0.1 collective-permute-start.7
  22.0 1.2 %collective-permute-done.7.refs_1_ = f32[128,128]{1,0:T(8,128)S(1)} collective-permute-done((f32[128,128]{1,0:T(8,128)S(1)}, f32[128,128]{1,0:T(8,128)S(1)}, u32[]{:S(2)}, u32[]{:S(2)}) %collective-permute-start.7) | collective-permute-done | bytes 65568 | tf_op jit(solution)/shard_map/ppermute | solution.py:272
  23.3 0.4 %collective-permute-start.10 = (f32[128,128]{1,0:T(8,128)S(1)}, f32[128,128]{1,0:T(8,128)S(1)}, u32[]{:S(2)}, u32[]{:S(2)}) collective-permute-start(f32[128,128]{1,0:T(8,128)S(1)} %sum.1.refs_0_), channel_id=1, source_target_pairs={{0,24},{4,28},{8,16},{12,20},{16,8},{20,12},{24,0},{28,4},{1,25},{... | collective-permute-start | bytes 196616 | tf_op jit(solution)/shard_map/ppermute | solution.py:272
  23.7 1.2 %collective-permute-start.9 = (f32[128,128]{1,0:T(8,128)S(1)}, f32[128,128]{1,0:T(8,128)S(1)}, u32[]{:S(2)}, u32[]{:S(2)}) collective-permute-start(f32[128,128]{1,0:T(8,128)S(1)} %sum.1.refs_0_), channel_id=1, source_target_pairs={{0,16},{4,20},{8,24},{12,28},{16,0},{20,4},{24,8},{28,12},{1,17},{... | collective-permute-start | bytes 196616 | tf_op jit(solution)/shard_map/ppermute | solution.py:272
  24.9 2.0 %collective-permute-start.8 = (f32[128,128]{1,0:T(8,128)S(1)}, f32[128,128]{1,0:T(8,128)S(1)}, u32[]{:S(2)}, u32[]{:S(2)}) collective-permute-start(f32[128,128]{1,0:T(8,128)S(1)} %sum.1.refs_0_), channel_id=1, source_target_pairs={{0,8},{4,12},{8,0},{12,4},{16,24},{20,28},{24,16},{28,20},{1,9},{5... | collective-permute-start | bytes 196616 | tf_op jit(solution)/shard_map/ppermute | solution.py:272
  26.9 2.3 %collective-permute-done.10.refs_3_ = f32[128,128]{1,0:T(8,128)S(1)} collective-permute-done((f32[128,128]{1,0:T(8,128)S(1)}, f32[128,128]{1,0:T(8,128)S(1)}, u32[]{:S(2)}, u32[]{:S(2)}) %collective-permute-start.10) | collective-permute-done | bytes 65568 | tf_op jit(solution)/shard_map/ppermute | solution.py:272
  29.1 0.0 collective-permute-done.8.refs_1_
  29.2 3.2 %rotate.1 = f32[32,512]{1,0:T(8,128)} custom-call(f32[128,128]{1,0:T(8,128)S(1)} %sum.1.refs_0_, f32[128,128]{1,0:T(8,128)S(1)} %collective-permute-done.8.refs_1_, f32[128,128]{1,0:T(8,128)S(1)} %collective-permute-done.9.refs_2_, f32[128,128]{1,0:T(8,128)S(1)} %collective-permute-done.10.refs_3_, bf16[2,128,512]{2,1,0:T(8,128)(2,1)S(1)} %get-tuple-element.12.refs_4_), custom_call_target="tpu_custom_call" | custom-call | tf_op jit(solution)/shard_map/rotate/pallas_call | solution.py:370
  (8 shorter events, 0.0 us)
Async XLA Ops:
  0.0 6.7 %copy-start = (f32[32,512]{1,0:T(8,128)S(1)}, f32[32,512]{1,0:T(8,128)}, u32[]{:S(2)}) copy-start(f32[32,512]{1,0:T(8,128)} %refs_5_.3) | copy-start | bytes 196612
  0.0 6.7 %collective-permute-start.2 = (f32[32,512]{1,0:T(8,128)}, f32[32,512]{1,0:T(8,128)S(1)}, u32[]{:S(2)}, u32[]{:S(2)}) collective-permute-start(f32[32,512]{1,0:T(8,128)} %refs_5_.3), channel_id=1, source_target_pairs={{0,4},{4,0},{8,12},{12,8},{16,20},{20,16},{24,28},{28,24},{1,5},{5... | collective-permute-start | bytes 196616 | tf_op jit(solution)/shard_map/ppermute | solution.py:272
  0.5 6.7 %collective-permute-start = (f32[32,512]{1,0:T(8,128)}, f32[32,512]{1,0:T(8,128)S(1)}, u32[]{:S(2)}, u32[]{:S(2)}) collective-permute-start(f32[32,512]{1,0:T(8,128)} %refs_5_.3), channel_id=1, source_target_pairs={{0,28},{4,8},{8,4},{12,16},{16,12},{20,24},{24,20},{28,0},{1,29},{... | collective-permute-start | bytes 196616 | tf_op jit(solution)/shard_map/ppermute | solution.py:291
  7.0 3.5 %collective-permute-start.3 = (f32[32,256]{1,0:T(8,128)S(1)}, f32[32,256]{1,0:T(8,128)S(1)}, u32[]{:S(2)}, u32[]{:S(2)}) collective-permute-start(f32[32,256]{1,0:T(8,128)S(1)} %first_near.1.refs_1_), channel_id=1, source_target_pairs={{0,4},{4,0},{8,12},{12,8},{16,20},{20,16},{24,28},{28,24},{1,5},{5... | collective-permute-start | bytes 98312 | tf_op jit(solution)/shard_map/ppermute | solution.py:272
  7.5 4.4 %collective-permute-start.1 = (f32[32,256]{1,0:T(8,128)S(1)}, f32[32,256]{1,0:T(8,128)S(1)}, u32[]{:S(2)}, u32[]{:S(2)}) collective-permute-start(f32[32,256]{1,0:T(8,128)S(1)} %first_far.1.refs_2_), channel_id=1, source_target_pairs={{0,28},{4,8},{8,4},{12,16},{16,12},{20,24},{24,20},{28,0},{1,29},{... | collective-permute-start | bytes 98312 | tf_op jit(solution)/shard_map/ppermute | solution.py:291
  12.2 6.7 %collective-permute-start.6 = (bf16[64,512]{1,0:T(8,128)(2,1)S(1)}, bf16[64,512]{1,0:T(8,128)(2,1)S(1)}, u32[]{:S(2)}, u32[]{:S(2)}) collective-permute-start(bf16[64,512]{1,0:T(8,128)(2,1)S(1)} %second_far.1.refs_0_), channel_id=1, source_target_pairs={{0,3},{1,2},{2,1},{3,0},{4,7},{5,6},{6,5},{7,4},{8,11},{9,10},{10,... | collective-permute-start | bytes 196616 | tf_op jit(solution)/shard_map/ppermute | solution.py:272
  15.9 4.9 %collective-permute-start.5 = (bf16[64,512]{1,0:T(8,128)(2,1)S(1)}, bf16[64,512]{1,0:T(8,128)(2,1)S(1)}, u32[]{:S(2)}, u32[]{:S(2)}) collective-permute-start(bf16[64,512]{1,0:T(8,128)(2,1)S(1)} %second_far.1.refs_0_), channel_id=1, source_target_pairs={{0,1},{1,0},{2,3},{3,2},{4,5},{5,4},{6,7},{7,6},{8,9},{9,8},{10,11... | collective-permute-start | bytes 196616 | tf_op jit(solution)/shard_map/ppermute | solution.py:272
  15.9 5.8 %collective-permute-start.4 = (bf16[64,512]{1,0:T(8,128)(2,1)S(1)}, bf16[64,512]{1,0:T(8,128)(2,1)S(1)}, u32[]{:S(2)}, u32[]{:S(2)}) collective-permute-start(bf16[64,512]{1,0:T(8,128)(2,1)S(1)} %second_far.1.refs_0_), channel_id=1, source_target_pairs={{0,2},{1,3},{2,0},{3,1},{4,6},{5,7},{6,4},{7,5},{8,10},{9,11},{10,... | collective-permute-start | bytes 196616 | tf_op jit(solution)/shard_map/ppermute | solution.py:272
  22.0 1.3 %collective-permute-start.7 = (f32[128,128]{1,0:T(8,128)S(1)}, f32[128,128]{1,0:T(8,128)S(1)}, u32[]{:S(2)}, u32[]{:S(2)}) collective-permute-start(f32[128,128]{1,0:T(8,128)S(1)} %get-tuple-element.11.refs_0_), channel_id=1, source_target_pairs={{0,4},{4,0},{8,12},{12,8},{16,20},{20,16},{24,28},{28,24},{1,5},{5... | collective-permute-start | bytes 196616 | tf_op jit(solution)/shard_map/ppermute | solution.py:272
  23.3 5.8 %collective-permute-start.10 = (f32[128,128]{1,0:T(8,128)S(1)}, f32[128,128]{1,0:T(8,128)S(1)}, u32[]{:S(2)}, u32[]{:S(2)}) collective-permute-start(f32[128,128]{1,0:T(8,128)S(1)} %sum.1.refs_0_), channel_id=1, source_target_pairs={{0,24},{4,28},{8,16},{12,20},{16,8},{20,12},{24,0},{28,4},{1,25},{... | collective-permute-start | bytes 196616 | tf_op jit(solution)/shard_map/ppermute | solution.py:272
  23.7 5.4 %collective-permute-start.9 = (f32[128,128]{1,0:T(8,128)S(1)}, f32[128,128]{1,0:T(8,128)S(1)}, u32[]{:S(2)}, u32[]{:S(2)}) collective-permute-start(f32[128,128]{1,0:T(8,128)S(1)} %sum.1.refs_0_), channel_id=1, source_target_pairs={{0,16},{4,20},{8,24},{12,28},{16,0},{20,4},{24,8},{28,12},{1,17},{... | collective-permute-start | bytes 196616 | tf_op jit(solution)/shard_map/ppermute | solution.py:272
  24.9 4.3 %collective-permute-start.8 = (f32[128,128]{1,0:T(8,128)S(1)}, f32[128,128]{1,0:T(8,128)S(1)}, u32[]{:S(2)}, u32[]{:S(2)}) collective-permute-start(f32[128,128]{1,0:T(8,128)S(1)} %sum.1.refs_0_), channel_id=1, source_target_pairs={{0,8},{4,12},{8,0},{12,4},{16,24},{20,28},{24,16},{28,20},{1,9},{5... | collective-permute-start | bytes 196616 | tf_op jit(solution)/shard_map/ppermute | solution.py:272
